TPU v7x, 256 devices: a whole 4x4x8 slice. The times are simulated.
256 devices in a mesh: node: 32 (over x, z), local: 8 (over y, core).
Axes of the slice: x: 4, y: 4, z: 8, core: 2. Of those that a mesh axis runs over, the one named last changes fastest.
Arguments:
- tokens: bfloat16 [32768, 3584], P(('node', 'local')), may hold values from -6 to 6
- expert_ids: int32 [32768, 4], P(('node', 'local')), may hold values from 0 to 127, as said below
- gate_weights: bfloat16 [32768, 4], P(('node', 'local')), may hold values from 0.099609375 to 1
- w_gate: bfloat16 [256, 3584, 512], P(('node', 'local')), may hold values from -0.09375 to 0.09375
- w_up: bfloat16 [256, 3584, 512], P(('node', 'local')), may hold values from -0.09375 to 0.09375
- w_down: bfloat16 [256, 512, 3584], P(('node', 'local')), may hold values from -0.1875 to 0.1875
Outputs:
- mixed: bfloat16 [32768, 3584], P(('node', 'local'))
Inputs may be any that keep to these rules, and one draw needn't show every extreme that they name: `expert_ids`: each row names 4 different experts, two on each of two different nodes (the node of expert e is e // 4); among the rows of one device no expert is named by more than 5 rows.
All inputs are finite; a program needn't handle non-finite values.
Results may differ from a plain program's by a relative error of at most 0.0065.
Values may be sent and summed in bfloat16 or wider, within the bound.
No kernel may reach another device: no remote copies, remote signals or barrier semaphores. Data moves between devices by JAX's collectives and lax.ppermute only.
A program may use at most 192 MiB of HBM per device.

v0:
```python
import functools
from typing import NamedTuple

import jax
import jax.numpy as jnp
from jax import lax
from jax.experimental import pallas as pl
from jax.experimental.pallas import tpu as pltpu
from jax.sharding import PartitionSpec as P

SLOTS = 5
EXPERTS = 4
NODE_ROWS = EXPERTS * SLOTS // 2
GROUP = 8


class Chunk(NamedTuple):
    start: int
    width: int
    pieces: int
    block: int

    @property
    def span(self):
        return self.width * self.pieces

    @property
    def group(self):
        return self.block * GROUP


OUT = (Chunk(0, 512, 3, 32), Chunk(1536, 512, 4, 40))
HOME = (Chunk(0, 384, 4, 40), Chunk(1536, 512, 4, 40))
BF = jnp.bfloat16
F32 = jnp.float32
VMEM = 63 << 20


def dot(a, b):
    return jnp.dot(a, b, preferred_element_type=F32)


def iota(shape, dim):
    return lax.broadcasted_iota(jnp.int32, shape, dim)


def steps(value, step, count):
    total = jnp.zeros_like(value)
    for i in range(1, count):
        total = total + jnp.where(value >= step * i, 1, 0)
    return total


def ones_where(mask):
    return jnp.where(mask, 1.0, 0.0).astype(F32)


def block_position(shape, dim, chunk):
    index = iota(shape, dim)
    node = steps(index, chunk.block, GROUP)
    inner = index - chunk.block * node
    piece = steps(inner, NODE_ROWS, chunk.pieces + 1)
    return node, piece, inner - NODE_ROWS * piece


def call(kernel, out_shape, cost, **kwargs):
    return pl.pallas_call(
        kernel,
        out_shape=out_shape,
        cost_estimate=pl.CostEstimate(flops=cost * 10**9, bytes_accessed=10**6, transcendentals=0),
        compiler_params=pltpu.CompilerParams(vmem_limit_bytes=VMEM),
        **kwargs,
    )


def node_code(ids, nodes):
    node = iota((nodes, ids.shape[1]), 0)
    hit = jnp.zeros(node.shape, F32)
    for k in range(ids.shape[0]):
        hit = jnp.maximum(hit, ones_where((ids[k : k + 1, :] >> 2) == node))
    tokens = ids.shape[1]
    before = ones_where(iota((tokens, tokens), 0) < iota((tokens, tokens), 1)).astype(BF)
    return jnp.where(hit > 0, dot(hit.astype(BF), before), -1.0)


def row_meta(ids, gates, code):
    top, tokens = ids.shape
    expert = iota((128, tokens), 0)
    hits = [ones_where(ids[k : k + 1, :] == expert) for k in range(top)]
    before = ones_where(iota((tokens, tokens), 0) < iota((tokens, tokens), 1)).astype(BF)
    rank = dot(functools.reduce(jnp.maximum, hits).astype(BF), before)
    items = [(ids[k : k + 1, :] + 1).astype(F32) for k in range(top)]
    items += [jnp.sum(hits[k] * rank, axis=0, keepdims=True) for k in range(top)]
    items += [gates[k : k + 1, :] for k in range(top)]
    table = jnp.concatenate(
        [jnp.broadcast_to(item, (16, tokens)) for item in items]
        + [jnp.zeros((256 - 16 * len(items), tokens), F32)],
        axis=0,
    )
    place = iota(table.shape, 0) & 15
    meta = jnp.zeros((code.shape[0], 256), F32)
    for r in range(NODE_ROWS):
        meta += lax.dot_general(
            ones_where(code == float(r)).astype(BF),
            jnp.where(place == r, table, 0.0).astype(BF),
            (((1,), (1,)), ((), ())),
            preferred_element_type=F32,
        )
    return meta.astype(BF)


def pack_kernel(chunk, with_meta, ids_ref, gates_ref, tok_ref, out_ref):
    ids = ids_ref[...]
    nodes = out_ref.shape[0] // chunk.block
    tokens = ids.shape[1]
    code = node_code(ids, nodes)
    inner = iota((chunk.block, tokens), 0)
    piece = steps(inner, NODE_ROWS, chunk.pieces + 1)
    row = (inner - NODE_ROWS * piece).astype(F32)
    wanted = [jnp.where(piece == q, row, -9.0) for q in range(chunk.pieces)]
    first = [chunk.start + q * chunk.width for q in range(chunk.pieces)]
    stacked = jnp.concatenate([tok_ref[:, at : at + chunk.width] for at in first], axis=0)
    if with_meta:
        meta = row_meta(ids, gates_ref[...].astype(F32), code)
        meta = jnp.concatenate([meta, jnp.zeros((nodes, chunk.width - 256), BF)], axis=1)
        node_of = steps(iota((chunk.group, nodes), 0), chunk.block, GROUP)
        inner_of = iota((chunk.group, nodes), 0) - chunk.block * node_of
    for g in range(nodes // GROUP):
        picks = []
        for q in range(chunk.pieces):
            picks.append(
                jnp.concatenate(
                    [ones_where(code[n : n + 1, :] == wanted[q]) for n in range(g * GROUP, (g + 1) * GROUP)],
                    axis=0,
                ).astype(BF)
            )
        rows = dot(jnp.concatenate(picks, axis=1), stacked)
        if with_meta:
            spot = (node_of + g * GROUP == iota((chunk.group, nodes), 1)) & (inner_of == chunk.pieces * NODE_ROWS)
            rows += dot(ones_where(spot).astype(BF), meta)
        out_ref[g * chunk.group : (g + 1) * chunk.group, :] = rows.astype(BF)


def pack(ids_t, gates_t, tokens, nodes, chunk, with_meta):
    return call(
        functools.partial(pack_kernel, chunk, with_meta),
        jax.ShapeDtypeStruct((nodes * chunk.block, chunk.width), BF),
        cost=5,
        name="pack_rows",
    )(ids_t, gates_t, tokens)


def expert_lanes(meta, expert, spread):
    ids = meta[:, :128]
    hit = ones_where(ids == (expert + 1).astype(F32))
    slot = dot((hit * (pltpu.roll(ids, 64, 1) + 1.0)).astype(BF), spread)
    gate = dot((hit * meta[:, 128:256]).astype(BF), spread)
    return slot, gate


def own_lane(values, node, g):
    part = values[g * GROUP : (g + 1) * GROUP, :]
    return jnp.sum(jnp.where(iota(part.shape, 0) == node, part, 0.0), axis=0, keepdims=True)


def lane_tables(chunk):
    node, piece, row = block_position((1, chunk.group), 1, chunk)
    lane = iota((128, chunk.group), 0)
    spread = ones_where(((lane & 15) == row) & (lane < 64)).astype(BF)
    return node, piece, spread


def row_target(chunk):
    row = iota((GROUP * SLOTS, chunk.group), 0)
    node = steps(row, SLOTS, GROUP)
    return (row + (8 - SLOTS) * node + 1).astype(F32)


def select_kernel(chunk, with_meta, where_ref, rows_ref, *out_refs):
    nodes = rows_ref.shape[0] // chunk.block
    width = chunk.width
    if with_meta:
        meta_ref, out_refs = out_refs[0], out_refs[1:]
        shape = (nodes, rows_ref.shape[0])
        spot = iota(shape, 1) == iota(shape, 0) * chunk.block + chunk.pieces * NODE_ROWS
        meta = dot(ones_where(spot).astype(BF), rows_ref[:, :256])
        meta_ref[...] = meta
    else:
        meta, out_refs = out_refs[0][...], out_refs[1:]
    node, piece, spread = lane_tables(chunk)
    target = row_target(chunk)
    slots = []
    for d in range(EXPERTS):
        expert = where_ref[0] * EXPERTS + ((where_ref[1] + d) & (EXPERTS - 1))
        slots.append(expert_lanes(meta, expert, spread)[0])
    shift = 8.0 * node.astype(F32)
    held = [[None] * EXPERTS for _ in range(chunk.pieces)]
    for g in range(nodes // GROUP):
        lines = [own_lane(slots[d], node, g) + shift for d in range(EXPERTS)]
        picks = []
        for q in range(chunk.pieces):
            for d in range(EXPERTS):
                line = jnp.where(piece == q, lines[d], -9.0)
                picks.append(ones_where(target == line))
        picked = dot(
            jnp.concatenate(picks, axis=0).astype(BF), rows_ref[g * chunk.group : (g + 1) * chunk.group, :]
        )
        height = GROUP * SLOTS
        for q in range(chunk.pieces):
            for d in range(EXPERTS):
                at = (q * EXPERTS + d) * height
                part = picked[at : at + height]
                if g % 2 == 0:
                    held[q][d] = part
                else:
                    both = jnp.concatenate([held[q][d], part], axis=0).astype(BF)
                    out_refs[d][(g - 1) * height : (g + 1) * height, q * width : (q + 1) * width] = both


def select(where, rows, meta, nodes, chunk):
    with_meta = meta is None
    shapes = [jax.ShapeDtypeStruct((nodes * SLOTS, chunk.span), BF)] * EXPERTS
    if with_meta:
        shapes = [jax.ShapeDtypeStruct((nodes, 256), F32)] + shapes
    out = call(
        functools.partial(select_kernel, chunk, with_meta),
        shapes,
        in_specs=[
            pl.BlockSpec(memory_space=pltpu.SMEM),
        ]
        + [pl.BlockSpec(memory_space=pltpu.VMEM)] * (1 if with_meta else 2),
        cost=20,
        name="select_rows",
    )(where, rows, *(() if with_meta else (meta,)))
    return (out[0], out[1:]) if with_meta else (None, out)


def mix_kernel(chunk, where_ref, meta_ref, *refs):
    out_ref, value_refs = refs[-1], refs[:-1]
    nodes = out_ref.shape[0] // chunk.block
    width = chunk.width
    meta = meta_ref[...]
    node, _, spread = lane_tables(chunk)
    target = row_target(chunk)
    tables = []
    for d in range(EXPERTS):
        expert = where_ref[0] * EXPERTS + ((where_ref[1] + d) & (EXPERTS - 1))
        tables.append(expert_lanes(meta, expert, spread))
    shift = 8.0 * node.astype(F32)
    _, out_piece, _ = block_position((chunk.group, width), 0, chunk)
    height = GROUP * SLOTS
    for g in range(nodes // GROUP):
        gated = []
        values = []
        for d in range(EXPERTS):
            line = own_lane(tables[d][0], node, g) + shift
            gate = own_lane(tables[d][1], node, g)
            gated.append(jnp.where(target == line, jnp.broadcast_to(gate, target.shape), 0.0))
            pair = value_refs[d][(g // 2) * 2 * height : (g // 2 + 1) * 2 * height, :].astype(F32)
            values.append(pair[(g % 2) * height : (g % 2 + 1) * height, :])
        share = lax.dot_general(
            jnp.concatenate(gated, axis=0).astype(BF),
            jnp.concatenate(values, axis=0).astype(BF),
            (((0,), (0,)), ((), ())),
            preferred_element_type=F32,
        )
        total = jnp.zeros((chunk.group, width), F32)
        for q in range(chunk.pieces):
            total = jnp.where(out_piece == q, share[:, q * width : (q + 1) * width], total)
        out_ref[g * chunk.group : (g + 1) * chunk.group, :] = total.astype(BF)


def mix(where, meta, values, nodes, chunk):
    return call(
        functools.partial(mix_kernel, chunk),
        jax.ShapeDtypeStruct((nodes * chunk.block, chunk.width), BF),
        in_specs=[pl.BlockSpec(memory_space=pltpu.SMEM)]
        + [pl.BlockSpec(memory_space=pltpu.VMEM)] * (1 + len(values)),
        cost=40,
        name="node_share",
    )(where, meta, *values)


def finish_kernel(chunk, ids_ref, home_ref, *refs):
    out_ref = refs[-1]
    at = 0
    if len(refs) > 1:
        at = chunk.start
        out_ref[:, :at] = refs[0][...]
    tokens, top = ids_ref.shape
    nodes = home_ref.shape[0] // chunk.block
    node = iota((tokens, nodes), 1)
    hit = jnp.zeros((tokens, nodes), F32)
    for k in range(top):
        hit = jnp.maximum(hit, ones_where((ids_ref[:, k : k + 1] >> 2) == node))
    before = ones_where(iota((tokens, tokens), 1) < iota((tokens, tokens), 0)).astype(BF)
    code = jnp.where(hit > 0, dot(before, hit.astype(BF)) + 1.0, 0.0).astype(BF)
    lane_node, piece, row = block_position((1, chunk.group), 1, chunk)
    total = jnp.zeros((chunk.pieces * tokens, chunk.width), F32)
    for g in range(nodes // GROUP):
        spread = ones_where(iota((nodes, chunk.group), 0) == lane_node + g * GROUP).astype(BF)
        lanes = dot(code, spread)
        picks = []
        for q in range(chunk.pieces):
            line = jnp.where(piece == q, row + 1, -9).astype(F32)
            picks.append(ones_where(lanes == line))
        total += dot(
            jnp.concatenate(picks, axis=0).astype(BF), home_ref[g * chunk.group : (g + 1) * chunk.group, :]
        )
    for q in range(chunk.pieces):
        column = at + q * chunk.width
        out_ref[:, column : column + chunk.width] = total[q * tokens : (q + 1) * tokens, :].astype(BF)


def finish(ids, home, chunk, *before):
    columns = chunk.span + (chunk.start if before else 0)
    return call(
        functools.partial(finish_kernel, chunk),
        jax.ShapeDtypeStruct((ids.shape[0], columns), BF),
        cost=6,
        name="sum_over_nodes",
    )(ids, home, *before)


def up_kernel(start, down_start, *refs):
    last = down_start is not None
    count = 2 * EXPERTS
    blocks, (gate_ref, up_ref), refs = refs[:count], refs[count : count + 2], refs[count + 2 :]
    if last:
        sums_in, down_ref, refs = refs[:2], refs[2], refs[3:]
        (hidden_ref, other_out), (x_ref, wg_ref, wu_ref, *sums, wd_ref, other_ref, sems) = refs[:2], refs[2:]
    else:
        outs, (x_ref, wg_ref, wu_ref, sems) = refs[:2], refs[2:]
    rows, span = blocks[0].shape
    band = pl.ds(start, span)
    used = iter(range(64))

    def begin(source, target):
        copy = pltpu.make_async_copy(source, target, sems.at[next(used)])
        copy.start()
        return copy

    weights = [begin(gate_ref.at[0, band, :], wg_ref), begin(up_ref.at[0, band, :], wu_ref)]
    order = [EXPERTS, EXPERTS + 2, 0, 2] if last else [0, 2, EXPERTS, EXPERTS + 2]
    loads = {}
    for i in order:
        at = pl.ds(i * rows, 2 * rows)
        loads[i] = [begin(blocks[k], x_ref.at[pl.ds(k * rows, rows), :]) for k in (i, i + 1)]
        if last:
            loads[i] += [begin(source.at[at, :], target.at[at, :]) for source, target in zip(sums_in, sums)]
            if i == order[1]:
                weights_down = begin(down_ref.at[0, :, pl.ds(down_start, other_ref.shape[1])], wd_ref)
    for copy in weights:
        copy.wait()
    for i in order:
        for copy in loads[i]:
            copy.wait()
        at = pl.ds(i * rows, 2 * rows)
        gate = dot(x_ref[at, :], wg_ref[...])
        up = dot(x_ref[at, :], wu_ref[...])
        if last:
            gate += sums[0][at, :]
            up += sums[1][at, :]
            hidden_ref[at, :] = ((gate / (1.0 + jnp.exp(-gate))) * up).astype(BF)
            if i == order[1]:
                weights_down.wait()
                other_ref[...] = dot(hidden_ref[pl.ds(EXPERTS * rows, EXPERTS * rows), :], wd_ref[...]).astype(BF)
                sent = begin(other_ref, other_out)
        else:
            outs[0][at, :] = gate
            outs[1][at, :] = up
    if last:
        sent.wait()


def up_step(blocks, w_gate, w_up, chunk):
    span = chunk.span
    rows = blocks[0].shape[0] * len(blocks)
    units = w_gate.shape[2]
    any_spec = pl.BlockSpec(memory_space=pl.ANY)
    args = list(blocks) + [w_gate, w_up]
    return call(
        functools.partial(up_kernel, chunk.start, None),
        [jax.ShapeDtypeStruct((rows, units), F32)] * 2,
        in_specs=[any_spec] * len(args),
        scratch_shapes=[
            pltpu.VMEM((rows, span), BF),
            pltpu.VMEM((span, units), BF),
            pltpu.VMEM((span, units), BF),
            pltpu.SemaphoreType.DMA((2 + len(blocks),)),
        ],
        cost=40,
        name="gate_up",
    )(*args)


def hidden_step(blocks, w_gate, w_up, sums, w_down, chunk, down_chunk):
    span, down_span = chunk.span, down_chunk.span
    rows = blocks[0].shape[0] * len(blocks)
    units = w_gate.shape[2]
    any_spec = pl.BlockSpec(memory_space=pl.ANY)
    args = list(blocks) + [w_gate, w_up] + list(sums) + [w_down]
    return call(
        functools.partial(up_kernel, chunk.start, down_chunk.start),
        [jax.ShapeDtypeStruct((rows, units), BF), jax.ShapeDtypeStruct((rows // 2, down_span), BF)],
        in_specs=[any_spec] * len(args),
        out_specs=[pl.BlockSpec(memory_space=pltpu.VMEM), any_spec],
        scratch_shapes=[
            pltpu.VMEM((rows, span), BF),
            pltpu.VMEM((span, units), BF),
            pltpu.VMEM((span, units), BF),
            pltpu.VMEM((rows, units), F32),
            pltpu.VMEM((rows, units), F32),
            pltpu.VMEM((units, down_span), BF),
            pltpu.VMEM((rows // 2, down_span), BF),
            pltpu.SemaphoreType.DMA((4 + 3 * len(blocks),)),
        ],
        cost=10,
        name="hidden_down",
    )(*args)


def down_other_kernel(hidden_ref, w_ref, out_ref):
    out_ref[...] = dot(hidden_ref[...], w_ref[0]).astype(BF)


def down_own_kernel(hidden_ref, w_ref, mate_ref, *out_refs):
    mine = dot(hidden_ref[...], w_ref[0]).astype(BF)
    value = (mine.astype(F32) + mate_ref[...].astype(F32)).astype(BF)
    rows = out_refs[0].shape[0]
    for d, out_ref in enumerate(out_refs):
        out_ref[...] = value[d * rows : (d + 1) * rows, :]


def down_other(hidden, w_down, chunk):
    start, span = chunk.start, chunk.span
    tile = 768 if start == 0 else 512
    rows, units = hidden.shape[0] // 2, hidden.shape[1]
    return call(
        down_other_kernel,
        jax.ShapeDtypeStruct((rows, span), BF),
        grid=(span // tile,),
        in_specs=[
            pl.BlockSpec((rows, units), lambda i: (1, 0)),
            pl.BlockSpec((1, units, tile), lambda i: (0, 0, start // tile + i)),
        ],
        out_specs=pl.BlockSpec((rows, tile), lambda i: (0, i)),
        cost=4,
        name="down_other",
    )(hidden, w_down)


def down_own(hidden, w_down, mate, chunk):
    start, span = chunk.start, chunk.span
    tile = 768 if start == 0 else 512
    rows, units = hidden.shape[0] // 2, hidden.shape[1]
    part = rows // EXPERTS
    return call(
        down_own_kernel,
        [jax.ShapeDtypeStruct((part, span), BF)] * EXPERTS,
        grid=(span // tile,),
        in_specs=[
            pl.BlockSpec((rows, units), lambda i: (0, 0)),
            pl.BlockSpec((1, units, tile), lambda i: (0, 0, start // tile + i)),
            pl.BlockSpec((rows, tile), lambda i: (0, i)),
        ],
        out_specs=[pl.BlockSpec((part, tile), lambda i: (0, i))] * EXPERTS,
        cost=10 if chunk.start == 0 else 4,
        name="down_own",
    )(hidden, w_down, mate)


def over_nodes(rows, nodes):
    cut = rows.reshape(nodes, rows.shape[0] // nodes, rows.shape[1])
    return lax.all_to_all(cut, "node", split_axis=0, concat_axis=0, tiled=True).reshape(rows.shape)


def along_y(block, distance):
    pairs = [(y * 2 + c, ((y + distance) % EXPERTS) * 2 + c) for y in range(EXPERTS) for c in range(2)]
    return lax.ppermute(block, "local", pairs)


def to_mate(block):
    return lax.ppermute(block, "local", [(i, i ^ 1) for i in range(2 * EXPERTS)])


def per_device(tokens, expert_ids, gate_weights, w_gate, w_up, w_down):
    nodes = lax.axis_size("node")
    where = jnp.stack([lax.axis_index("node"), lax.axis_index("local") // 2]).astype(jnp.int32)
    ids_t = expert_ids.T
    gates_t = gate_weights.T
    packed = [pack(ids_t, gates_t, tokens, nodes, chunk, chunk is OUT[0]) for chunk in OUT]
    packed[1], where = lax.optimization_barrier((packed[1], where))
    arrived = [over_nodes(rows, nodes) for rows in packed]
    meta, blocks = select(where, arrived[0], None, nodes, OUT[0])
    own = [blocks[0]] + [along_y(blocks[d], d) for d in range(1, EXPERTS)]
    near = to_mate(blocks[0])
    _, blocks = select(where, arrived[1], meta, nodes, OUT[1])
    own, near, blocks = lax.optimization_barrier((own, near, blocks))
    later = [along_y(blocks[d], d) for d in range(1, EXPERTS)]
    later_near = to_mate(blocks[0])
    sums = up_step(own + [near] + [to_mate(block) for block in own[1:]], w_gate, w_up, OUT[0])
    later, sums = lax.optimization_barrier((later, sums))
    own = [blocks[0]] + later
    hidden, other = hidden_step(
        own + [later_near] + [to_mate(block) for block in later], w_gate, w_up, sums, w_down, OUT[1], HOME[0]
    )
    mate = to_mate(other)
    later_mate = to_mate(down_other(hidden, w_down, HOME[1]))
    values = down_own(hidden, w_down, mate, HOME[0])
    back = [values[0]] + [along_y(values[d], -d) for d in range(1, EXPERTS)]
    values = down_own(hidden, w_down, later_mate, HOME[1])
    back, values = lax.optimization_barrier((back, values))
    later_back = [values[0]] + [along_y(values[d], -d) for d in range(1, EXPERTS)]
    home = over_nodes(mix(where, meta, back, nodes, HOME[0]), nodes)
    later_home = over_nodes(mix(where, meta, later_back, nodes, HOME[1]), nodes)
    return finish(expert_ids, later_home, HOME[1], finish(expert_ids, home, HOME[0]))


def solution(mesh):
    rows = P(("node", "local"), None)
    cube = P(("node", "local"), None, None)
    return jax.shard_map(
        per_device,
        mesh=mesh,
        in_specs=(rows, rows, rows, cube, cube, cube),
        out_specs=rows,
        check_vma=False,
    )
```

profile of v0, /device:TPU:32, one launch (start us, length us, event | category | flops | bytes accessed | tf_op | source)
XLA Modules:
  0.0 256.9 jit_solution(16301178567933632684)
XLA Ops:
  0.0 4.1 %pack_rows.3 = bf16[1024,512]{1,0:T(8,128)(2,1)} custom-call(s32[4,128]{1,0:T(4,128)} %bitcast.17, bf16[4,128]{1,0:T(4,128)(2,1)} %bitcast.19, bf16[128,3584]{1,0:T(8,128)(2,1)} %tok_ref.3), custom_call_target="tpu_custom_call" | custom-call | flops 5000000000 | bytes 1000000 | tf_op jit(solution)/shard_map/pack_rows/pallas_call | solution.py:145
  4.1 11.2 %all-to-all-start = ((bf16[32,32,512]{2,1,0:T(8,128)(2,1)}), bf16[32,32,512]{2,1,0:T(8,128)(2,1)}, u32[]{:S(2)}, u32[]{:S(2)}) async-start(bf16[32,32,512]{2,1,0:T(8,128)(2,1)} %bitcast.14), calls=%async_computation | async-start | bytes 2097152 | tf_op jit(solution)/shard_map/all_to_all | solution.py:475
  15.9 3.3 %pack_rows.2 = bf16[1280,512]{1,0:T(8,128)(2,1)} custom-call(s32[4,128]{1,0:T(4,128)} %bitcast.18, bf16[4,128]{1,0:T(4,128)(2,1)} %bitcast.20, bf16[128,3584]{1,0:T(8,128)(2,1)} %tok_ref.3), custom_call_target="tpu_custom_call" | custom-call | flops 5000000000 | bytes 1000000 | tf_op jit(solution)/shard_map/pack_rows/pallas_call | solution.py:145
  19.2 24.7 %all-to-all-done = bf16[32,32,512]{2,1,0:T(8,128)(2,1)} async-done(((bf16[32,32,512]{2,1,0:T(8,128)(2,1)}), bf16[32,32,512]{2,1,0:T(8,128)(2,1)}, u32[]{:S(2)}, u32[]{:S(2)}) %all-to-all-start) | async-done | bytes 1048608 | tf_op jit(solution)/shard_map/all_to_all | solution.py:475
  43.9 5.2 %all-to-all-start.1 = ((bf16[32,40,512]{2,1,0:T(8,128)(2,1)}), bf16[32,40,512]{2,1,0:T(8,128)(2,1)}, u32[]{:S(2)}, u32[]{:S(2)}) async-start(bf16[32,40,512]{2,1,0:T(8,128)(2,1)} %bitcast.12), calls=%async_computation.1 | async-start | bytes 2621440 | tf_op jit(solution)/shard_map/all_to_all | solution.py:475
  49.2 3.7 %select_rows.2 = (f32[32,256]{1,0:T(8,128)}, bf16[160,1536]{1,0:T(8,128)(2,1)}, bf16[160,1536]{1,0:T(8,128)(2,1)}, bf16[160,1536]{1,0:T(8,128)(2,1)}, bf16[160,1536]{1,0:T(8,128)(2,1)}) custom-call(s32[2]{0:T(128)} %pad_add_fusion.where_ref, bf16[1024,512]{1,0:T(8,128)(2,1)} %bitcast.5.rows_ref), custom_call_target="tpu_custom_call" | custom-call | flops 20000000000 | bytes 1000000 | tf_op jit(solution)/shard_map/select_rows/pallas_call | solution.py:225
  54.4 2.9 %collective-permute-start.1 = (bf16[160,1536]{1,0:T(8,128)(2,1)}, bf16[160,1536]{1,0:T(8,128)(2,1)}, u32[]{:S(2)}, u32[]{:S(2)}) collective-permute-start(bf16[160,1536]{1,0:T(8,128)(2,1)} %get-tuple-element.54), channel_id=1, source_target_pairs={{0,4},{1,5},{2,6},{3,7},{4,0},{5,1},{6,2},{7,3},{8,12},{9,13},{10,... | collective-permute-start | bytes 1474568 | tf_op jit(solution)/shard_map/ppermute | solution.py:480
  58.7 23.9 %all-to-all-done.1 = bf16[32,40,512]{2,1,0:T(8,128)(2,1)} async-done(((bf16[32,40,512]{2,1,0:T(8,128)(2,1)}), bf16[32,40,512]{2,1,0:T(8,128)(2,1)}, u32[]{:S(2)}, u32[]{:S(2)}) %all-to-all-start.1) | async-done | bytes 1310752 | tf_op jit(solution)/shard_map/all_to_all | solution.py:475
  82.6 4.5 %select_rows.3 = (bf16[160,2048]{1,0:T(8,128)(2,1)}, bf16[160,2048]{1,0:T(8,128)(2,1)}, bf16[160,2048]{1,0:T(8,128)(2,1)}, bf16[160,2048]{1,0:T(8,128)(2,1)}) custom-call(s32[2]{0:T(128)} %pad_add_fusion.where_ref, bf16[1280,512]{1,0:T(8,128)(2,1)} %bitcast.7.rows_ref, f32[32,256]{1,0:T(8,128)} %get-tuple-element.51.out_refs_0_.meta_ref), custom_call_target="tpu_custom_call" | custom-call | flops 20000000000 | bytes 1000000 | tf_op jit(solution)/shard_map/select_rows/pallas_call | solution.py:225
  87.9 1.6 collective-permute-start.4
  89.5 2.9 %collective-permute-start.5 = (bf16[160,2048]{1,0:T(8,128)(2,1)}, bf16[160,2048]{1,0:T(8,128)(2,1)}, u32[]{:S(2)}, u32[]{:S(2)}) collective-permute-start(bf16[160,2048]{1,0:T(8,128)(2,1)} %get-tuple-element.63), channel_id=1, source_target_pairs={{0,4},{1,5},{2,6},{3,7},{4,0},{5,1},{6,2},{7,3},{8,12},{9,13},{10,... | collective-permute-start | bytes 1966088 | tf_op jit(solution)/shard_map/ppermute | solution.py:480
  93.8 8.8 %gate_up.1 = (f32[1280,512]{1,0:T(8,128)}, f32[1280,512]{1,0:T(8,128)}) custom-call(bf16[160,1536]{1,0:T(8,128)(2,1)} %get-tuple-element.65.refs_0_, bf16[160,1536]{1,0:T(8,128)(2,1)} %collective-permute-done.refs_1_, bf16[160,1536]{1,0:T(8,128)(2,1)} %collective-permute-done.1.refs_2_, bf16[160,1536]{1,0:T(8,128)(2,1)} %collective-permute-done.2.refs_3_, ...), custom_call_target="tpu_custom_call" | custom-call | flops 40000000000 | bytes 1000000 | tf_op jit(solution)/shard_map/gate_up/pallas_call | solution.py:382
  102.5 4.0 %collective-permute-done.4.refs_1_ = bf16[160,2048]{1,0:T(8,128)(2,1)S(1)} collective-permute-done((bf16[160,2048]{1,0:T(8,128)(2,1)}, bf16[160,2048]{1,0:T(8,128)(2,1)S(1)}, u32[]{:S(2)}, u32[]{:S(2)}) %collective-permute-start.4) | collective-permute-done | bytes 655392 | tf_op jit(solution)/shard_map/ppermute | solution.py:480
  106.6 15.3 %collective-permute-done.5.refs_2_ = bf16[160,2048]{1,0:T(8,128)(2,1)} collective-permute-done((bf16[160,2048]{1,0:T(8,128)(2,1)}, bf16[160,2048]{1,0:T(8,128)(2,1)}, u32[]{:S(2)}, u32[]{:S(2)}) %collective-permute-start.5) | collective-permute-done | bytes 655392 | tf_op jit(solution)/shard_map/ppermute | solution.py:480
  122.4 2.5 collective-permute-done.11.refs_5_
  126.6 11.5 %hidden_down.1 = (bf16[1280,512]{1,0:T(8,128)(2,1)}, bf16[640,1536]{1,0:T(8,128)(2,1)}) custom-call(bf16[160,2048]{1,0:T(8,128)(2,1)} %get-tuple-element.61.refs_0_, bf16[160,2048]{1,0:T(8,128)(2,1)} %copy-done.2, bf16[160,2048]{1,0:T(8,128)(2,1)} %collective-permute-done.5.refs_2_, bf16[160,2048]{1,0:T(8,128)(2,1)} %collective-permute-done.6.refs_3_, ...), custom_call_target="tpu_custom_call" | custom-call | flops 10000000000 | bytes 1000000 | tf_op jit(solution)/shard_map/hidden_down/pallas_call | solution.py:403
  138.6 5.2 %down_other.1 = bf16[640,2048]{1,0:T(8,128)(2,1)} custom-call(bf16[1280,512]{1,0:T(8,128)(2,1)} %get-tuple-element.77.hidden_ref, bf16[1,512,3584]{2,1,0:T(8,128)(2,1)} %w_ref.5), custom_call_target="tpu_custom_call" | custom-call | flops 4000000000 | bytes 1000000 | tf_op jit(solution)/shard_map/down_other/pallas_call | solution.py:439
  143.9 3.9 %down_own.2 = (bf16[160,1536]{1,0:T(8,128)(2,1)}, bf16[160,1536]{1,0:T(8,128)(2,1)}, bf16[160,1536]{1,0:T(8,128)(2,1)}, bf16[160,1536]{1,0:T(8,128)(2,1)}) custom-call(bf16[1280,512]{1,0:T(8,128)(2,1)} %get-tuple-element.77.hidden_ref, bf16[1,512,3584]{2,1,0:T(8,128)(2,1)} %w_ref.5, bf16[640,1536]{1,0:T(8,128)(2,1)} %collective-permute-done.14.mate_ref), custom_call_target="tpu_custom_call" | custom-call | flops 10000000000 | bytes 1000000 | tf_op jit(solution)/shard_map/down_own/pallas_call | solution.py:458
  147.8 2.1 collective-permute-start.15
  151.8 5.3 %down_own.3 = (bf16[160,2048]{1,0:T(8,128)(2,1)}, bf16[160,2048]{1,0:T(8,128)(2,1)}, bf16[160,2048]{1,0:T(8,128)(2,1)}, bf16[160,2048]{1,0:T(8,128)(2,1)}) custom-call(bf16[1280,512]{1,0:T(8,128)(2,1)} %get-tuple-element.77.hidden_ref, bf16[1,512,3584]{2,1,0:T(8,128)(2,1)} %w_ref.5, bf16[640,2048]{1,0:T(8,128)(2,1)} %collective-permute-done.18.mate_ref), custom_call_target="tpu_custom_call" | custom-call | flops 4000000000 | bytes 1000000 | tf_op jit(solution)/shard_map/down_own/pallas_call | solution.py:458
  157.1 14.7 %collective-permute-done.15.refs_1_ = bf16[160,1536]{1,0:T(8,128)(2,1)S(1)} collective-permute-done((bf16[160,1536]{1,0:T(8,128)(2,1)}, bf16[160,1536]{1,0:T(8,128)(2,1)S(1)}, u32[]{:S(2)}, u32[]{:S(2)}) %collective-permute-start.15) | collective-permute-done | bytes 491552 | tf_op jit(solution)/shard_map/ppermute | solution.py:480
  171.8 3.7 %collective-permute-done.17.refs_3_ = bf16[160,1536]{1,0:T(8,128)(2,1)} collective-permute-done((bf16[160,1536]{1,0:T(8,128)(2,1)}, bf16[160,1536]{1,0:T(8,128)(2,1)}, u32[]{:S(2)}, u32[]{:S(2)}) %collective-permute-start.17) | collective-permute-done | bytes 491552 | tf_op jit(solution)/shard_map/ppermute | solution.py:480
  178.0 4.0 %node_share.3 = bf16[1280,384]{1,0:T(8,128)(2,1)} custom-call(s32[2]{0:T(128)} %pad_add_fusion.where_ref, f32[32,256]{1,0:T(8,128)} %get-tuple-element.51.out_refs_0_.meta_ref, bf16[160,1536]{1,0:T(8,128)(2,1)} %get-tuple-element.91.refs_0_, bf16[160,1536]{1,0:T(8,128)(2,1)} %copy-done.6, bf16[160,1536]{1,0:T(8,128)(2,1)} %copy-done.7, ...), custom_call_target="tpu_custom_call" | custom-call | flops 40000000000 | bytes 1000000 | tf_op jit(solution)/shard_map/node_share/pallas_call | solution.py:274
  182.0 5.5 %all-to-all-start.3 = ((bf16[32,40,384]{2,1,0:T(8,128)(2,1)}), bf16[32,40,384]{2,1,0:T(8,128)(2,1)S(1)}, u32[]{:S(2)}, u32[]{:S(2)}) async-start(bf16[32,40,384]{2,1,0:T(8,128)(2,1)} %bitcast.16), calls=%async_computation.3 | async-start | bytes 1966080 | tf_op jit(solution)/shard_map/all_to_all | solution.py:475
  187.5 5.9 %collective-permute-done.19.refs_1_ = bf16[160,2048]{1,0:T(8,128)(2,1)} collective-permute-done((bf16[160,2048]{1,0:T(8,128)(2,1)}, bf16[160,2048]{1,0:T(8,128)(2,1)}, u32[]{:S(2)}, u32[]{:S(2)}) %collective-permute-start.19) | collective-permute-done | bytes 655392 | tf_op jit(solution)/shard_map/ppermute | solution.py:480
  193.4 2.2 collective-permute-done.20.refs_2_
  195.6 12.4 %collective-permute-done.21.refs_3_ = bf16[160,2048]{1,0:T(8,128)(2,1)} collective-permute-done((bf16[160,2048]{1,0:T(8,128)(2,1)}, bf16[160,2048]{1,0:T(8,128)(2,1)}, u32[]{:S(2)}, u32[]{:S(2)}) %collective-permute-start.21) | collective-permute-done | bytes 655392 | tf_op jit(solution)/shard_map/ppermute | solution.py:480
  208.0 4.7 %node_share.2 = bf16[1280,512]{1,0:T(8,128)(2,1)} custom-call(s32[2]{0:T(128)} %pad_add_fusion.where_ref, f32[32,256]{1,0:T(8,128)} %get-tuple-element.51.out_refs_0_.meta_ref, bf16[160,2048]{1,0:T(8,128)(2,1)} %get-tuple-element.87.refs_0_, bf16[160,2048]{1,0:T(8,128)(2,1)} %collective-permute-done.19.refs_1_, ...), custom_call_target="tpu_custom_call" | custom-call | flops 40000000000 | bytes 1000000 | tf_op jit(solution)/shard_map/node_share/pallas_call | solution.py:274
  214.1 5.1 %all-to-all-start.2 = ((bf16[32,40,512]{2,1,0:T(8,128)(2,1)}), bf16[32,40,512]{2,1,0:T(8,128)(2,1)}, u32[]{:S(2)}, u32[]{:S(2)}) async-start(bf16[32,40,512]{2,1,0:T(8,128)(2,1)} %bitcast.13), calls=%async_computation.2 | async-start | bytes 2621440 | tf_op jit(solution)/shard_map/all_to_all | solution.py:475
  219.9 3.8 %sum_over_nodes.2.refs_0_ = bf16[128,1536]{1,0:T(8,128)(2,1)} custom-call(s32[128,4]{1,0:T(8,128)} %copy.8.ids_ref, bf16[1280,384]{1,0:T(8,128)(2,1)} %bitcast.15), custom_call_target="tpu_custom_call" | custom-call | flops 6000000000 | bytes 1000000 | tf_op jit(solution)/shard_map/sum_over_nodes/pallas_call | solution.py:317
  223.7 28.9 %all-to-all-done.2 = bf16[32,40,512]{2,1,0:T(8,128)(2,1)} async-done(((bf16[32,40,512]{2,1,0:T(8,128)(2,1)}), bf16[32,40,512]{2,1,0:T(8,128)(2,1)}, u32[]{:S(2)}, u32[]{:S(2)}) %all-to-all-start.2) | async-done | bytes 1310752 | tf_op jit(solution)/shard_map/all_to_all | solution.py:475
  252.6 4.3 %sum_over_nodes.3 = bf16[128,3584]{1,0:T(8,128)(2,1)} custom-call(s32[128,4]{1,0:T(8,128)} %copy.8.ids_ref, bf16[1280,512]{1,0:T(8,128)(2,1)} %bitcast.9.home_ref, bf16[128,1536]{1,0:T(8,128)(2,1)} %sum_over_nodes.2.refs_0_), custom_call_target="tpu_custom_call" | custom-call | flops 6000000000 | bytes 1000000 | tf_op jit(solution)/shard_map/sum_over_nodes/pallas_call | solution.py:317
  (51 shorter events, 15.1 us)
Async XLA Ops:
  4.1 39.8 %all-to-all-start = ((bf16[32,32,512]{2,1,0:T(8,128)(2,1)}), bf16[32,32,512]{2,1,0:T(8,128)(2,1)}, u32[]{:S(2)}, u32[]{:S(2)}) async-start(bf16[32,32,512]{2,1,0:T(8,128)(2,1)} %bitcast.14), calls=%async_computation | async-start | bytes 2097152 | tf_op jit(solution)/shard_map/all_to_all | solution.py:475
  43.9 38.7 %all-to-all-start.1 = ((bf16[32,40,512]{2,1,0:T(8,128)(2,1)}), bf16[32,40,512]{2,1,0:T(8,128)(2,1)}, u32[]{:S(2)}, u32[]{:S(2)}) async-start(bf16[32,40,512]{2,1,0:T(8,128)(2,1)} %bitcast.12), calls=%async_computation.1 | async-start | bytes 2621440 | tf_op jit(solution)/shard_map/all_to_all | solution.py:475
  52.8 34.3 %collective-permute-start.3 = (bf16[160,1536]{1,0:T(8,128)(2,1)}, bf16[160,1536]{1,0:T(8,128)(2,1)S(1)}, u32[]{:S(2)}, u32[]{:S(2)}) collective-permute-start(bf16[160,1536]{1,0:T(8,128)(2,1)} %get-tuple-element.65.refs_0_), channel_id=1, source_target_pairs={{0,1},{1,0},{2,3},{3,2},{4,5},{5,4},{6,7},{7,6},{8,9},{9,8},{10,11... | collective-permute-start | bytes 1474568 | tf_op jit(solution)/shard_map/ppermute | solution.py:484
  52.8 34.3 %collective-permute-start = (bf16[160,1536]{1,0:T(8,128)(2,1)}, bf16[160,1536]{1,0:T(8,128)(2,1)}, u32[]{:S(2)}, u32[]{:S(2)}) collective-permute-start(bf16[160,1536]{1,0:T(8,128)(2,1)} %get-tuple-element.53), channel_id=1, source_target_pairs={{0,2},{1,3},{2,4},{3,5},{4,6},{5,7},{6,0},{7,1},{8,10},{9,11},{10,... | collective-permute-start | bytes 1474568 | tf_op jit(solution)/shard_map/ppermute | solution.py:480
  54.4 32.7 %collective-permute-start.1 = (bf16[160,1536]{1,0:T(8,128)(2,1)}, bf16[160,1536]{1,0:T(8,128)(2,1)}, u32[]{:S(2)}, u32[]{:S(2)}) collective-permute-start(bf16[160,1536]{1,0:T(8,128)(2,1)} %get-tuple-element.54), channel_id=1, source_target_pairs={{0,4},{1,5},{2,6},{3,7},{4,0},{5,1},{6,2},{7,3},{8,12},{9,13},{10,... | collective-permute-start | bytes 1474568 | tf_op jit(solution)/shard_map/ppermute | solution.py:480
  57.3 29.8 %collective-permute-start.2 = (bf16[160,1536]{1,0:T(8,128)(2,1)}, bf16[160,1536]{1,0:T(8,128)(2,1)}, u32[]{:S(2)}, u32[]{:S(2)}) collective-permute-start(bf16[160,1536]{1,0:T(8,128)(2,1)} %get-tuple-element.55), channel_id=1, source_target_pairs={{0,6},{1,7},{2,0},{3,1},{4,2},{5,3},{6,4},{7,5},{8,14},{9,15},{10,... | collective-permute-start | bytes 1474568 | tf_op jit(solution)/shard_map/ppermute | solution.py:480
  87.2 5.3 %collective-permute-start.7 = (bf16[160,1536]{1,0:T(8,128)(2,1)}, bf16[160,1536]{1,0:T(8,128)(2,1)}, u32[]{:S(2)}, u32[]{:S(2)}) collective-permute-start(bf16[160,1536]{1,0:T(8,128)(2,1)} %collective-permute-done.refs_1_), channel_id=1, source_target_pairs={{0,1},{1,0},{2,3},{3,2},{4,5},{5,4},{6,7},{7,6},{8,9},{9,8},{10,11... | collective-permute-start | bytes 1474568 | tf_op jit(solution)/shard_map/ppermute | solution.py:484
  87.3 6.5 %collective-permute-start.8 = (bf16[160,1536]{1,0:T(8,128)(2,1)}, bf16[160,1536]{1,0:T(8,128)(2,1)}, u32[]{:S(2)}, u32[]{:S(2)}) collective-permute-start(bf16[160,1536]{1,0:T(8,128)(2,1)} %collective-permute-done.1.refs_2_), channel_id=1, source_target_pairs={{0,1},{1,0},{2,3},{3,2},{4,5},{5,4},{6,7},{7,6},{8,9},{9,8},{10,11... | collective-permute-start | bytes 1474568 | tf_op jit(solution)/shard_map/ppermute | solution.py:484
  87.9 5.9 %collective-permute-start.9 = (bf16[160,1536]{1,0:T(8,128)(2,1)}, bf16[160,1536]{1,0:T(8,128)(2,1)}, u32[]{:S(2)}, u32[]{:S(2)}) collective-permute-start(bf16[160,1536]{1,0:T(8,128)(2,1)} %collective-permute-done.2.refs_3_), channel_id=1, source_target_pairs={{0,1},{1,0},{2,3},{3,2},{4,5},{5,4},{6,7},{7,6},{8,9},{9,8},{10,11... | collective-permute-start | bytes 1474568 | tf_op jit(solution)/shard_map/ppermute | solution.py:484
  87.9 18.6 %collective-permute-start.4 = (bf16[160,2048]{1,0:T(8,128)(2,1)}, bf16[160,2048]{1,0:T(8,128)(2,1)S(1)}, u32[]{:S(2)}, u32[]{:S(2)}) collective-permute-start(bf16[160,2048]{1,0:T(8,128)(2,1)} %get-tuple-element.62), channel_id=1, source_target_pairs={{0,2},{1,3},{2,4},{3,5},{4,6},{5,7},{6,0},{7,1},{8,10},{9,11},{10,... | collective-permute-start | bytes 1966088 | tf_op jit(solution)/shard_map/ppermute | solution.py:480
  89.5 32.4 %collective-permute-start.5 = (bf16[160,2048]{1,0:T(8,128)(2,1)}, bf16[160,2048]{1,0:T(8,128)(2,1)}, u32[]{:S(2)}, u32[]{:S(2)}) collective-permute-start(bf16[160,2048]{1,0:T(8,128)(2,1)} %get-tuple-element.63), channel_id=1, source_target_pairs={{0,4},{1,5},{2,6},{3,7},{4,0},{5,1},{6,2},{7,3},{8,12},{9,13},{10,... | collective-permute-start | bytes 1966088 | tf_op jit(solution)/shard_map/ppermute | solution.py:480
  92.4 29.5 %collective-permute-start.6 = (bf16[160,2048]{1,0:T(8,128)(2,1)}, bf16[160,2048]{1,0:T(8,128)(2,1)}, u32[]{:S(2)}, u32[]{:S(2)}) collective-permute-start(bf16[160,2048]{1,0:T(8,128)(2,1)} %get-tuple-element.64), channel_id=1, source_target_pairs={{0,6},{1,7},{2,0},{3,1},{4,2},{5,3},{6,4},{7,5},{8,14},{9,15},{10,... | collective-permute-start | bytes 1966088 | tf_op jit(solution)/shard_map/ppermute | solution.py:480
  93.8 28.6 %collective-permute-start.10 = (bf16[160,2048]{1,0:T(8,128)(2,1)}, bf16[160,2048]{1,0:T(8,128)(2,1)}, u32[]{:S(2)}, u32[]{:S(2)}) collective-permute-start(bf16[160,2048]{1,0:T(8,128)(2,1)} %get-tuple-element.61.refs_0_), channel_id=1, source_target_pairs={{0,1},{1,0},{2,3},{3,2},{4,5},{5,4},{6,7},{7,6},{8,9},{9,8},{10,11... | collective-permute-start | bytes 1966088 | tf_op jit(solution)/shard_map/ppermute | solution.py:484
  106.6 20.1 %copy-start.2 = (bf16[160,2048]{1,0:T(8,128)(2,1)}, bf16[160,2048]{1,0:T(8,128)(2,1)S(1)}, u32[]{:S(2)}) copy-start(bf16[160,2048]{1,0:T(8,128)(2,1)S(1)} %collective-permute-done.4.refs_1_) | copy-start | bytes 1966084
  121.9 3.0 %collective-permute-start.11 = (bf16[160,2048]{1,0:T(8,128)(2,1)S(1)}, bf16[160,2048]{1,0:T(8,128)(2,1)S(1)}, u32[]{:S(2)}, u32[]{:S(2)}) collective-permute-start(bf16[160,2048]{1,0:T(8,128)(2,1)S(1)} %collective-permute-done.4.refs_1_), channel_id=1, source_target_pairs={{0,1},{1,0},{2,3},{3,2},{4,5},{5,4},{6,7},{7,6},{8,9},{9,8},{10,11... | collective-permute-start | bytes 1966088 | tf_op jit(solution)/shard_map/ppermute | solution.py:484
  121.9 3.8 %collective-permute-start.12 = (bf16[160,2048]{1,0:T(8,128)(2,1)}, bf16[160,2048]{1,0:T(8,128)(2,1)S(1)}, u32[]{:S(2)}, u32[]{:S(2)}) collective-permute-start(bf16[160,2048]{1,0:T(8,128)(2,1)} %collective-permute-done.5.refs_2_), channel_id=1, source_target_pairs={{0,1},{1,0},{2,3},{3,2},{4,5},{5,4},{6,7},{7,6},{8,9},{9,8},{10,11... | collective-permute-start | bytes 1966088 | tf_op jit(solution)/shard_map/ppermute | solution.py:484
  122.4 4.2 %collective-permute-start.13 = (bf16[160,2048]{1,0:T(8,128)(2,1)}, bf16[160,2048]{1,0:T(8,128)(2,1)}, u32[]{:S(2)}, u32[]{:S(2)}) collective-permute-start(bf16[160,2048]{1,0:T(8,128)(2,1)} %collective-permute-done.6.refs_3_), channel_id=1, source_target_pairs={{0,1},{1,0},{2,3},{3,2},{4,5},{5,4},{6,7},{7,6},{8,9},{9,8},{10,11... | collective-permute-start | bytes 1966088 | tf_op jit(solution)/shard_map/ppermute | solution.py:484
  125.7 0.9 copy-start.4
  138.2 5.8 %collective-permute-start.14 = (bf16[640,1536]{1,0:T(8,128)(2,1)}, bf16[640,1536]{1,0:T(8,128)(2,1)}, u32[]{:S(2)}, u32[]{:S(2)}) collective-permute-start(bf16[640,1536]{1,0:T(8,128)(2,1)} %get-tuple-element.78), channel_id=1, source_target_pairs={{0,1},{1,0},{2,3},{3,2},{4,5},{5,4},{6,7},{7,6},{8,9},{9,8},{10,11... | collective-permute-start | bytes 5898248 | tf_op jit(solution)/shard_map/ppermute | solution.py:484
  143.7 8.1 %collective-permute-start.18 = (bf16[640,2048]{1,0:T(8,128)(2,1)}, bf16[640,2048]{1,0:T(8,128)(2,1)}, u32[]{:S(2)}, u32[]{:S(2)}) collective-permute-start(bf16[640,2048]{1,0:T(8,128)(2,1)} %down_other.1), channel_id=1, source_target_pairs={{0,1},{1,0},{2,3},{3,2},{4,5},{5,4},{6,7},{7,6},{8,9},{9,8},{10,11... | collective-permute-start | bytes 7864328 | tf_op jit(solution)/shard_map/ppermute | solution.py:484
  147.8 23.9 %collective-permute-start.15 = (bf16[160,1536]{1,0:T(8,128)(2,1)}, bf16[160,1536]{1,0:T(8,128)(2,1)S(1)}, u32[]{:S(2)}, u32[]{:S(2)}) collective-permute-start(bf16[160,1536]{1,0:T(8,128)(2,1)} %get-tuple-element.80), channel_id=1, source_target_pairs={{0,6},{1,7},{2,0},{3,1},{4,2},{5,3},{6,4},{7,5},{8,14},{9,15},{10,... | collective-permute-start | bytes 1474568 | tf_op jit(solution)/shard_map/ppermute | solution.py:480
  149.9 21.9 %collective-permute-start.16 = (bf16[160,1536]{1,0:T(8,128)(2,1)}, bf16[160,1536]{1,0:T(8,128)(2,1)S(1)}, u32[]{:S(2)}, u32[]{:S(2)}) collective-permute-start(bf16[160,1536]{1,0:T(8,128)(2,1)} %get-tuple-element.81), channel_id=1, source_target_pairs={{0,4},{1,5},{2,6},{3,7},{4,0},{5,1},{6,2},{7,3},{8,12},{9,13},{10,... | collective-permute-start | bytes 1474568 | tf_op jit(solution)/shard_map/ppermute | solution.py:480
  151.1 24.4 %collective-permute-start.17 = (bf16[160,1536]{1,0:T(8,128)(2,1)}, bf16[160,1536]{1,0:T(8,128)(2,1)}, u32[]{:S(2)}, u32[]{:S(2)}) collective-permute-start(bf16[160,1536]{1,0:T(8,128)(2,1)} %get-tuple-element.82), channel_id=1, source_target_pairs={{0,2},{1,3},{2,4},{3,5},{4,6},{5,7},{6,0},{7,1},{8,10},{9,11},{10,... | collective-permute-start | bytes 1474568 | tf_op jit(solution)/shard_map/ppermute | solution.py:480
  171.8 6.2 %copy-start.6 = (bf16[160,1536]{1,0:T(8,128)(2,1)}, bf16[160,1536]{1,0:T(8,128)(2,1)S(1)}, u32[]{:S(2)}) copy-start(bf16[160,1536]{1,0:T(8,128)(2,1)S(1)} %collective-permute-done.15.refs_1_) | copy-start | bytes 1474564
  171.8 6.2 %copy-start.7 = (bf16[160,1536]{1,0:T(8,128)(2,1)}, bf16[160,1536]{1,0:T(8,128)(2,1)S(1)}, u32[]{:S(2)}) copy-start(bf16[160,1536]{1,0:T(8,128)(2,1)S(1)} %collective-permute-done.16.refs_2_) | copy-start | bytes 1474564
  175.5 17.9 %collective-permute-start.19 = (bf16[160,2048]{1,0:T(8,128)(2,1)}, bf16[160,2048]{1,0:T(8,128)(2,1)}, u32[]{:S(2)}, u32[]{:S(2)}) collective-permute-start(bf16[160,2048]{1,0:T(8,128)(2,1)} %get-tuple-element.88), channel_id=1, source_target_pairs={{0,6},{1,7},{2,0},{3,1},{4,2},{5,3},{6,4},{7,5},{8,14},{9,15},{10,... | collective-permute-start | bytes 1966088 | tf_op jit(solution)/shard_map/ppermute | solution.py:480
  176.1 19.5 %collective-permute-start.20 = (bf16[160,2048]{1,0:T(8,128)(2,1)}, bf16[160,2048]{1,0:T(8,128)(2,1)}, u32[]{:S(2)}, u32[]{:S(2)}) collective-permute-start(bf16[160,2048]{1,0:T(8,128)(2,1)} %get-tuple-element.89), channel_id=1, source_target_pairs={{0,4},{1,5},{2,6},{3,7},{4,0},{5,1},{6,2},{7,3},{8,12},{9,13},{10,... | collective-permute-start | bytes 1966088 | tf_op jit(solution)/shard_map/ppermute | solution.py:480
  177.2 30.8 %collective-permute-start.21 = (bf16[160,2048]{1,0:T(8,128)(2,1)}, bf16[160,2048]{1,0:T(8,128)(2,1)}, u32[]{:S(2)}, u32[]{:S(2)}) collective-permute-start(bf16[160,2048]{1,0:T(8,128)(2,1)} %get-tuple-element.90), channel_id=1, source_target_pairs={{0,2},{1,3},{2,4},{3,5},{4,6},{5,7},{6,0},{7,1},{8,10},{9,11},{10,... | collective-permute-start | bytes 1966088 | tf_op jit(solution)/shard_map/ppermute | solution.py:480
  182.0 32.1 %all-to-all-start.3 = ((bf16[32,40,384]{2,1,0:T(8,128)(2,1)}), bf16[32,40,384]{2,1,0:T(8,128)(2,1)S(1)}, u32[]{:S(2)}, u32[]{:S(2)}) async-start(bf16[32,40,384]{2,1,0:T(8,128)(2,1)} %bitcast.16), calls=%async_computation.3 | async-start | bytes 1966080 | tf_op jit(solution)/shard_map/all_to_all | solution.py:475
  212.7 6.5 %copy-start.1 = (s32[128,4]{0,1:T(4,128)S(1)}, s32[128,4]{0,1:T(4,128)}, u32[]{:S(2)}) copy-start(s32[128,4]{0,1:T(4,128)} %param.7) | copy-start | bytes 6148
  214.1 5.9 %copy-start = (bf16[32,40,384]{2,1,0:T(8,128)(2,1)}, bf16[32,40,384]{2,1,0:T(8,128)(2,1)S(1)}, u32[]{:S(2)}) copy-start(bf16[32,40,384]{2,1,0:T(8,128)(2,1)S(1)} %all-to-all-done.3) | copy-start | bytes 2949124
  214.1 38.5 %all-to-all-start.2 = ((bf16[32,40,512]{2,1,0:T(8,128)(2,1)}), bf16[32,40,512]{2,1,0:T(8,128)(2,1)}, u32[]{:S(2)}, u32[]{:S(2)}) async-start(bf16[32,40,512]{2,1,0:T(8,128)(2,1)} %bitcast.13), calls=%async_computation.2 | async-start | bytes 2621440 | tf_op jit(solution)/shard_map/all_to_all | solution.py:475
  (2 other events, 1.6 us)
where the time goes:
time: 259 us; the launch traced here: 257 us
  waiting for transfers between devices  140 us (54%)
  Pallas kernels  67 us (26%)
  starting transfers between devices  47 us (18%)
  local copies, waits for them, and re-layouts  2.63 us (1%)
    all_to_all x4, waiting for transfers between devices, over_nodes(): lax.all_to_all(cut, 'node', split_axis=0, concat_axis=0, tiled=True)  78.9 us
    ppermute x12, waiting for transfers between devices, along_y(): return lax.ppermute(block, 'local', pairs)  58.2 us
    all_to_all x4, starting transfers between devices, over_nodes(): lax.all_to_all(cut, 'node', split_axis=0, concat_axis=0, tiled=True)  27 us
    ppermute x12, starting transfers between devices, along_y(): return lax.ppermute(block, 'local', pairs)  18.2 us
    pallas_call x1, Pallas kernels, hidden_step(): call(functools.partial(up_kernel, chunk.start, down_chunk.start), [jax.Sh...  11.5 us
    pallas_call x2, Pallas kernels, down_own(): call(down_own_kernel, [jax.ShapeDtypeStruct((part, span), BF)] * EXPERTS,...  9.2 us
    pallas_call x1, Pallas kernels, up_step(): call(functools.partial(up_kernel, chunk.start, None), [jax.ShapeDtypeStru...  8.75 us
    pallas_call x2, Pallas kernels, mix(): call(functools.partial(mix_kernel, chunk), jax.ShapeDtypeStruct((nodes *...  8.65 us
  transfers between devices with their start and end apart: 26, of which 12 were waited for; matrix products, arithmetic and copies ran while one was open for 1% of the time, Pallas kernels for 18%

commit v1 on v0

--- a/solution.py
+++ b/solution.py
@@ -389,7 +389,7 @@
             pltpu.VMEM((span, units), BF),
             pltpu.SemaphoreType.DMA((2 + len(blocks),)),
         ],
-        cost=40,
+        cost=1,
         name="gate_up",
     )(*args)
 
@@ -510,7 +510,6 @@
     values = down_own(hidden, w_down, mate, HOME[0])
     back = [values[0]] + [along_y(values[d], -d) for d in range(1, EXPERTS)]
     values = down_own(hidden, w_down, later_mate, HOME[1])
-    back, values = lax.optimization_barrier((back, values))
     later_back = [values[0]] + [along_y(values[d], -d) for d in range(1, EXPERTS)]
     home = over_nodes(mix(where, meta, back, nodes, HOME[0]), nodes)
     later_home = over_nodes(mix(where, meta, later_back, nodes, HOME[1]), nodes)

time: 259 us -> 256 us (0.988)
  waiting for transfers between devices: 140 us -> 137 us
    ppermute x12, waiting for transfers between devices: 58.2 us -> 49.3 us  [along_y(): return lax.ppermute(block, 'local', pairs)]
    all_to_all x4, waiting for transfers between devices: 78.9 us -> 82.5 us  [over_nodes(): lax.all_to_all(cut, 'node', split_axis=0, concat_axis=0, tiled=True)]
    ppermute x10, waiting for transfers between devices: 2.5 us -> 5.5 us  [to_mate(): lax.ppermute(block, 'local', [(i, i ^ 1) for i in range(2 * EXPERTS)])]
  transfers between devices with their start and end apart: 26 -> 26, of which waited for: 12 -> 15; matrix products, arithmetic and copies ran while one was open for 1% -> 1% of each run, Pallas kernels for 18% -> 18%
where the time goes in v1:
time: 256 us; the launch traced here: 255 us
  waiting for transfers between devices  137 us (54%)
  Pallas kernels  67 us (26%)
  starting transfers between devices  48.3 us (19%)
    all_to_all x4, waiting for transfers between devices, over_nodes(): lax.all_to_all(cut, 'node', split_axis=0, concat_axis=0, tiled=True)  82.5 us
    ppermute x12, waiting for transfers between devices, along_y(): return lax.ppermute(block, 'local', pairs)  49.3 us
    all_to_all x4, starting transfers between devices, over_nodes(): lax.all_to_all(cut, 'node', split_axis=0, concat_axis=0, tiled=True)  27.1 us
    ppermute x12, starting transfers between devices, along_y(): return lax.ppermute(block, 'local', pairs)  19.3 us
    pallas_call x1, Pallas kernels, hidden_step(): call(functools.partial(up_kernel, chunk.start, down_chunk.start), [jax.Sh...  11.5 us
    pallas_call x2, Pallas kernels, down_own(): call(down_own_kernel, [jax.ShapeDtypeStruct((part, span), BF)] * EXPERTS,...  9.24 us
    pallas_call x1, Pallas kernels, up_step(): call(functools.partial(up_kernel, chunk.start, None), [jax.ShapeDtypeStru...  8.75 us
    pallas_call x2, Pallas kernels, mix(): call(functools.partial(mix_kernel, chunk), jax.ShapeDtypeStruct((nodes *...  8.65 us
  transfers between devices with their start and end apart: 26, of which 15 were waited for; matrix products, arithmetic and copies ran while one was open for 1% of the time, Pallas kernels for 18%

profile of v1, /device:TPU:32, one launch (start us, length us, event | category | flops | bytes accessed | tf_op | source)
XLA Modules:
  0.0 254.9 jit_solution(10307777061410141245)
XLA Ops:
  0.0 4.1 %pack_rows.3 = bf16[1024,512]{1,0:T(8,128)(2,1)} custom-call(s32[4,128]{1,0:T(4,128)} %bitcast.17, bf16[4,128]{1,0:T(4,128)(2,1)} %bitcast.19, bf16[128,3584]{1,0:T(8,128)(2,1)} %tok_ref.3), custom_call_target="tpu_custom_call" | custom-call | flops 5000000000 | bytes 1000000 | tf_op jit(solution)/shard_map/pack_rows/pallas_call | solution.py:145
  4.1 11.2 %all-to-all-start = ((bf16[32,32,512]{2,1,0:T(8,128)(2,1)}), bf16[32,32,512]{2,1,0:T(8,128)(2,1)}, u32[]{:S(2)}, u32[]{:S(2)}) async-start(bf16[32,32,512]{2,1,0:T(8,128)(2,1)} %bitcast.14), calls=%async_computation | async-start | bytes 2097152 | tf_op jit(solution)/shard_map/all_to_all | solution.py:475
  16.0 3.3 %pack_rows.2 = bf16[1280,512]{1,0:T(8,128)(2,1)} custom-call(s32[4,128]{1,0:T(4,128)} %bitcast.18, bf16[4,128]{1,0:T(4,128)(2,1)} %bitcast.20, bf16[128,3584]{1,0:T(8,128)(2,1)} %tok_ref.3), custom_call_target="tpu_custom_call" | custom-call | flops 5000000000 | bytes 1000000 | tf_op jit(solution)/shard_map/pack_rows/pallas_call | solution.py:145
  19.3 24.6 %all-to-all-done = bf16[32,32,512]{2,1,0:T(8,128)(2,1)} async-done(((bf16[32,32,512]{2,1,0:T(8,128)(2,1)}), bf16[32,32,512]{2,1,0:T(8,128)(2,1)}, u32[]{:S(2)}, u32[]{:S(2)}) %all-to-all-start) | async-done | bytes 1048608 | tf_op jit(solution)/shard_map/all_to_all | solution.py:475
  43.9 5.2 %all-to-all-start.1 = ((bf16[32,40,512]{2,1,0:T(8,128)(2,1)}), bf16[32,40,512]{2,1,0:T(8,128)(2,1)}, u32[]{:S(2)}, u32[]{:S(2)}) async-start(bf16[32,40,512]{2,1,0:T(8,128)(2,1)} %bitcast.12), calls=%async_computation.1 | async-start | bytes 2621440 | tf_op jit(solution)/shard_map/all_to_all | solution.py:475
  49.2 3.6 %select_rows.2 = (f32[32,256]{1,0:T(8,128)}, bf16[160,1536]{1,0:T(8,128)(2,1)}, bf16[160,1536]{1,0:T(8,128)(2,1)}, bf16[160,1536]{1,0:T(8,128)(2,1)}, bf16[160,1536]{1,0:T(8,128)(2,1)}) custom-call(s32[2]{0:T(128)} %pad_add_fusion.where_ref, bf16[1024,512]{1,0:T(8,128)(2,1)} %bitcast.5.rows_ref), custom_call_target="tpu_custom_call" | custom-call | flops 20000000000 | bytes 1000000 | tf_op jit(solution)/shard_map/select_rows/pallas_call | solution.py:225
  54.4 2.9 %collective-permute-start.1 = (bf16[160,1536]{1,0:T(8,128)(2,1)}, bf16[160,1536]{1,0:T(8,128)(2,1)}, u32[]{:S(2)}, u32[]{:S(2)}) collective-permute-start(bf16[160,1536]{1,0:T(8,128)(2,1)} %get-tuple-element.46), channel_id=1, source_target_pairs={{0,4},{1,5},{2,6},{3,7},{4,0},{5,1},{6,2},{7,3},{8,12},{9,13},{10,... | collective-permute-start | bytes 1474568 | tf_op jit(solution)/shard_map/ppermute | solution.py:480
  58.6 24.0 %all-to-all-done.1 = bf16[32,40,512]{2,1,0:T(8,128)(2,1)} async-done(((bf16[32,40,512]{2,1,0:T(8,128)(2,1)}), bf16[32,40,512]{2,1,0:T(8,128)(2,1)}, u32[]{:S(2)}, u32[]{:S(2)}) %all-to-all-start.1) | async-done | bytes 1310752 | tf_op jit(solution)/shard_map/all_to_all | solution.py:475
  82.6 4.5 %select_rows.3 = (bf16[160,2048]{1,0:T(8,128)(2,1)}, bf16[160,2048]{1,0:T(8,128)(2,1)}, bf16[160,2048]{1,0:T(8,128)(2,1)}, bf16[160,2048]{1,0:T(8,128)(2,1)}) custom-call(s32[2]{0:T(128)} %pad_add_fusion.where_ref, bf16[1280,512]{1,0:T(8,128)(2,1)} %bitcast.7.rows_ref, f32[32,256]{1,0:T(8,128)} %get-tuple-element.43.out_refs_0_.meta_ref), custom_call_target="tpu_custom_call" | custom-call | flops 20000000000 | bytes 1000000 | tf_op jit(solution)/shard_map/select_rows/pallas_call | solution.py:225
  87.2 1.7 collective-permute-start.4
  88.9 2.9 %collective-permute-start.5 = (bf16[160,2048]{1,0:T(8,128)(2,1)}, bf16[160,2048]{1,0:T(8,128)(2,1)}, u32[]{:S(2)}, u32[]{:S(2)}) collective-permute-start(bf16[160,2048]{1,0:T(8,128)(2,1)} %get-tuple-element.55), channel_id=1, source_target_pairs={{0,4},{1,5},{2,6},{3,7},{4,0},{5,1},{6,2},{7,3},{8,12},{9,13},{10,... | collective-permute-start | bytes 1966088 | tf_op jit(solution)/shard_map/ppermute | solution.py:480
  96.3 8.7 %gate_up.1 = (f32[1280,512]{1,0:T(8,128)}, f32[1280,512]{1,0:T(8,128)}) custom-call(bf16[160,1536]{1,0:T(8,128)(2,1)} %get-tuple-element.57.refs_0_, bf16[160,1536]{1,0:T(8,128)(2,1)} %copy-done.2, bf16[160,1536]{1,0:T(8,128)(2,1)} %collective-permute-done.1.refs_2_, bf16[160,1536]{1,0:T(8,128)(2,1)} %collective-permute-done.2.refs_3_, ...), custom_call_target="tpu_custom_call" | custom-call | flops 1000000000 | bytes 1000000 | tf_op jit(solution)/shard_map/gate_up/pallas_call | solution.py:382
  106.0 15.2 %collective-permute-done.5.refs_2_ = bf16[160,2048]{1,0:T(8,128)(2,1)} collective-permute-done((bf16[160,2048]{1,0:T(8,128)(2,1)}, bf16[160,2048]{1,0:T(8,128)(2,1)}, u32[]{:S(2)}, u32[]{:S(2)}) %collective-permute-start.5) | collective-permute-done | bytes 655392 | tf_op jit(solution)/shard_map/ppermute | solution.py:480
  121.7 2.7 %collective-permute-done.11.refs_5_ = bf16[160,2048]{1,0:T(8,128)(2,1)S(1)} collective-permute-done((bf16[160,2048]{1,0:T(8,128)(2,1)}, bf16[160,2048]{1,0:T(8,128)(2,1)S(1)}, u32[]{:S(2)}, u32[]{:S(2)}) %collective-permute-start.11) | collective-permute-done | bytes 655392 | tf_op jit(solution)/shard_map/ppermute | solution.py:484
  125.5 11.5 %hidden_down.1 = (bf16[1280,512]{1,0:T(8,128)(2,1)}, bf16[640,1536]{1,0:T(8,128)(2,1)}) custom-call(bf16[160,2048]{1,0:T(8,128)(2,1)} %get-tuple-element.53.refs_0_, bf16[160,2048]{1,0:T(8,128)(2,1)} %collective-permute-done.4.refs_1_, bf16[160,2048]{1,0:T(8,128)(2,1)} %collective-permute-done.5.refs_2_, bf16[160,2048]{1,0:T(8,128)(2,1)} %collective-permute-done.6.refs_3_, ...), custom_call_target="tpu_custom_call" | custom-call | flops 10000000000 | bytes 1000000 | tf_op jit(solution)/shard_map/hidden_down/pallas_call | solution.py:403
  137.3 5.2 %down_other.1 = bf16[640,2048]{1,0:T(8,128)(2,1)} custom-call(bf16[1280,512]{1,0:T(8,128)(2,1)} %get-tuple-element.69.hidden_ref, bf16[1,512,3584]{2,1,0:T(8,128)(2,1)} %w_ref.5), custom_call_target="tpu_custom_call" | custom-call | flops 4000000000 | bytes 1000000 | tf_op jit(solution)/shard_map/down_other/pallas_call | solution.py:439
  142.8 3.9 %down_own.3 = (bf16[160,1536]{1,0:T(8,128)(2,1)}, bf16[160,1536]{1,0:T(8,128)(2,1)}, bf16[160,1536]{1,0:T(8,128)(2,1)}, bf16[160,1536]{1,0:T(8,128)(2,1)}) custom-call(bf16[1280,512]{1,0:T(8,128)(2,1)} %get-tuple-element.69.hidden_ref, bf16[1,512,3584]{2,1,0:T(8,128)(2,1)} %w_ref.5, bf16[640,1536]{1,0:T(8,128)(2,1)} %collective-permute-done.18.mate_ref), custom_call_target="tpu_custom_call" | custom-call | flops 10000000000 | bytes 1000000 | tf_op jit(solution)/shard_map/down_own/pallas_call | solution.py:458
  146.8 2.1 collective-permute-start.19
  150.8 5.3 %down_own.2 = (bf16[160,2048]{1,0:T(8,128)(2,1)}, bf16[160,2048]{1,0:T(8,128)(2,1)}, bf16[160,2048]{1,0:T(8,128)(2,1)}, bf16[160,2048]{1,0:T(8,128)(2,1)}) custom-call(bf16[1280,512]{1,0:T(8,128)(2,1)} %get-tuple-element.69.hidden_ref, bf16[1,512,3584]{2,1,0:T(8,128)(2,1)} %w_ref.5, bf16[640,2048]{1,0:T(8,128)(2,1)} %collective-permute-done.14.mate_ref), custom_call_target="tpu_custom_call" | custom-call | flops 4000000000 | bytes 1000000 | tf_op jit(solution)/shard_map/down_own/pallas_call | solution.py:458
  156.1 2.4 collective-permute-start.15
  159.7 11.4 %collective-permute-done.19.refs_1_ = bf16[160,1536]{1,0:T(8,128)(2,1)S(1)} collective-permute-done((bf16[160,1536]{1,0:T(8,128)(2,1)}, bf16[160,1536]{1,0:T(8,128)(2,1)S(1)}, u32[]{:S(2)}, u32[]{:S(2)}) %collective-permute-start.19) | collective-permute-done | bytes 491552 | tf_op jit(solution)/shard_map/ppermute | solution.py:480
  171.1 4.3 %collective-permute-done.21.refs_3_ = bf16[160,1536]{1,0:T(8,128)(2,1)} collective-permute-done((bf16[160,1536]{1,0:T(8,128)(2,1)}, bf16[160,1536]{1,0:T(8,128)(2,1)}, u32[]{:S(2)}, u32[]{:S(2)}) %collective-permute-start.21) | collective-permute-done | bytes 491552 | tf_op jit(solution)/shard_map/ppermute | solution.py:480
  175.4 4.0 %node_share.3 = bf16[1280,384]{1,0:T(8,128)(2,1)} custom-call(s32[2]{0:T(128)} %pad_add_fusion.where_ref, f32[32,256]{1,0:T(8,128)} %get-tuple-element.43.out_refs_0_.meta_ref, bf16[160,1536]{1,0:T(8,128)(2,1)} %get-tuple-element.75.refs_0_, bf16[160,1536]{1,0:T(8,128)(2,1)} %copy-done.6, bf16[160,1536]{1,0:T(8,128)(2,1)} %copy-done.7, ...), custom_call_target="tpu_custom_call" | custom-call | flops 40000000000 | bytes 1000000 | tf_op jit(solution)/shard_map/node_share/pallas_call | solution.py:274
  179.4 5.5 %all-to-all-start.3 = ((bf16[32,40,384]{2,1,0:T(8,128)(2,1)}), bf16[32,40,384]{2,1,0:T(8,128)(2,1)S(1)}, u32[]{:S(2)}, u32[]{:S(2)}) async-start(bf16[32,40,384]{2,1,0:T(8,128)(2,1)} %bitcast.16), calls=%async_computation.3 | async-start | bytes 1966080 | tf_op jit(solution)/shard_map/all_to_all | solution.py:475
  184.8 13.7 %collective-permute-done.15.refs_1_ = bf16[160,2048]{1,0:T(8,128)(2,1)} collective-permute-done((bf16[160,2048]{1,0:T(8,128)(2,1)}, bf16[160,2048]{1,0:T(8,128)(2,1)}, u32[]{:S(2)}, u32[]{:S(2)}) %collective-permute-start.15) | collective-permute-done | bytes 655392 | tf_op jit(solution)/shard_map/ppermute | solution.py:480
  198.6 3.7 %collective-permute-done.17.refs_3_ = bf16[160,2048]{1,0:T(8,128)(2,1)} collective-permute-done((bf16[160,2048]{1,0:T(8,128)(2,1)}, bf16[160,2048]{1,0:T(8,128)(2,1)}, u32[]{:S(2)}, u32[]{:S(2)}) %collective-permute-start.17) | collective-permute-done | bytes 655392 | tf_op jit(solution)/shard_map/ppermute | solution.py:480
  202.2 4.7 %node_share.2 = bf16[1280,512]{1,0:T(8,128)(2,1)} custom-call(s32[2]{0:T(128)} %pad_add_fusion.where_ref, f32[32,256]{1,0:T(8,128)} %get-tuple-element.43.out_refs_0_.meta_ref, bf16[160,2048]{1,0:T(8,128)(2,1)} %get-tuple-element.70.refs_0_, bf16[160,2048]{1,0:T(8,128)(2,1)} %collective-permute-done.15.refs_1_, ...), custom_call_target="tpu_custom_call" | custom-call | flops 40000000000 | bytes 1000000 | tf_op jit(solution)/shard_map/node_share/pallas_call | solution.py:274
  206.9 5.0 %all-to-all-done.3 = bf16[32,40,384]{2,1,0:T(8,128)(2,1)S(1)} async-done(((bf16[32,40,384]{2,1,0:T(8,128)(2,1)}), bf16[32,40,384]{2,1,0:T(8,128)(2,1)S(1)}, u32[]{:S(2)}, u32[]{:S(2)}) %all-to-all-start.3) | async-done | bytes 983072 | tf_op jit(solution)/shard_map/all_to_all | solution.py:475
  211.9 5.2 %all-to-all-start.2 = ((bf16[32,40,512]{2,1,0:T(8,128)(2,1)}), bf16[32,40,512]{2,1,0:T(8,128)(2,1)}, u32[]{:S(2)}, u32[]{:S(2)}) async-start(bf16[32,40,512]{2,1,0:T(8,128)(2,1)} %bitcast.13), calls=%async_computation.2 | async-start | bytes 2621440 | tf_op jit(solution)/shard_map/all_to_all | solution.py:475
  217.9 3.8 %sum_over_nodes.2.refs_0_ = bf16[128,1536]{1,0:T(8,128)(2,1)} custom-call(s32[128,4]{1,0:T(8,128)} %copy.8.ids_ref, bf16[1280,384]{1,0:T(8,128)(2,1)} %bitcast.15), custom_call_target="tpu_custom_call" | custom-call | flops 6000000000 | bytes 1000000 | tf_op jit(solution)/shard_map/sum_over_nodes/pallas_call | solution.py:317
  221.7 28.9 %all-to-all-done.2 = bf16[32,40,512]{2,1,0:T(8,128)(2,1)} async-done(((bf16[32,40,512]{2,1,0:T(8,128)(2,1)}), bf16[32,40,512]{2,1,0:T(8,128)(2,1)}, u32[]{:S(2)}, u32[]{:S(2)}) %all-to-all-start.2) | async-done | bytes 1310752 | tf_op jit(solution)/shard_map/all_to_all | solution.py:475
  250.5 4.3 %sum_over_nodes.3 = bf16[128,3584]{1,0:T(8,128)(2,1)} custom-call(s32[128,4]{1,0:T(8,128)} %copy.8.ids_ref, bf16[1280,512]{1,0:T(8,128)(2,1)} %bitcast.9.home_ref, bf16[128,1536]{1,0:T(8,128)(2,1)} %sum_over_nodes.2.refs_0_), custom_call_target="tpu_custom_call" | custom-call | flops 6000000000 | bytes 1000000 | tf_op jit(solution)/shard_map/sum_over_nodes/pallas_call | solution.py:317
  (51 shorter events, 15.2 us)
Async XLA Ops:
  4.1 39.8 %all-to-all-start = ((bf16[32,32,512]{2,1,0:T(8,128)(2,1)}), bf16[32,32,512]{2,1,0:T(8,128)(2,1)}, u32[]{:S(2)}, u32[]{:S(2)}) async-start(bf16[32,32,512]{2,1,0:T(8,128)(2,1)} %bitcast.14), calls=%async_computation | async-start | bytes 2097152 | tf_op jit(solution)/shard_map/all_to_all | solution.py:475
  43.9 38.7 %all-to-all-start.1 = ((bf16[32,40,512]{2,1,0:T(8,128)(2,1)}), bf16[32,40,512]{2,1,0:T(8,128)(2,1)}, u32[]{:S(2)}, u32[]{:S(2)}) async-start(bf16[32,40,512]{2,1,0:T(8,128)(2,1)} %bitcast.12), calls=%async_computation.1 | async-start | bytes 2621440 | tf_op jit(solution)/shard_map/all_to_all | solution.py:475
  52.8 34.3 %collective-permute-start.3 = (bf16[160,1536]{1,0:T(8,128)(2,1)}, bf16[160,1536]{1,0:T(8,128)(2,1)S(1)}, u32[]{:S(2)}, u32[]{:S(2)}) collective-permute-start(bf16[160,1536]{1,0:T(8,128)(2,1)} %get-tuple-element.57.refs_0_), channel_id=1, source_target_pairs={{0,1},{1,0},{2,3},{3,2},{4,5},{5,4},{6,7},{7,6},{8,9},{9,8},{10,11... | collective-permute-start | bytes 1474568 | tf_op jit(solution)/shard_map/ppermute | solution.py:484
  52.8 34.3 %collective-permute-start = (bf16[160,1536]{1,0:T(8,128)(2,1)}, bf16[160,1536]{1,0:T(8,128)(2,1)S(1)}, u32[]{:S(2)}, u32[]{:S(2)}) collective-permute-start(bf16[160,1536]{1,0:T(8,128)(2,1)} %get-tuple-element.45), channel_id=1, source_target_pairs={{0,2},{1,3},{2,4},{3,5},{4,6},{5,7},{6,0},{7,1},{8,10},{9,11},{10,... | collective-permute-start | bytes 1474568 | tf_op jit(solution)/shard_map/ppermute | solution.py:480
  54.4 32.7 %collective-permute-start.1 = (bf16[160,1536]{1,0:T(8,128)(2,1)}, bf16[160,1536]{1,0:T(8,128)(2,1)}, u32[]{:S(2)}, u32[]{:S(2)}) collective-permute-start(bf16[160,1536]{1,0:T(8,128)(2,1)} %get-tuple-element.46), channel_id=1, source_target_pairs={{0,4},{1,5},{2,6},{3,7},{4,0},{5,1},{6,2},{7,3},{8,12},{9,13},{10,... | collective-permute-start | bytes 1474568 | tf_op jit(solution)/shard_map/ppermute | solution.py:480
  57.3 29.9 %collective-permute-start.2 = (bf16[160,1536]{1,0:T(8,128)(2,1)}, bf16[160,1536]{1,0:T(8,128)(2,1)}, u32[]{:S(2)}, u32[]{:S(2)}) collective-permute-start(bf16[160,1536]{1,0:T(8,128)(2,1)} %get-tuple-element.47), channel_id=1, source_target_pairs={{0,6},{1,7},{2,0},{3,1},{4,2},{5,3},{6,4},{7,5},{8,14},{9,15},{10,... | collective-permute-start | bytes 1474568 | tf_op jit(solution)/shard_map/ppermute | solution.py:480
  87.1 9.2 %copy-start.1 = (bf16[160,1536]{1,0:T(8,128)(2,1)}, bf16[160,1536]{1,0:T(8,128)(2,1)S(1)}, u32[]{:S(2)}) copy-start(bf16[160,1536]{1,0:T(8,128)(2,1)S(1)} %collective-permute-done.3.refs_4_) | copy-start | bytes 1474564
  87.1 9.2 %copy-start.2 = (bf16[160,1536]{1,0:T(8,128)(2,1)}, bf16[160,1536]{1,0:T(8,128)(2,1)S(1)}, u32[]{:S(2)}) copy-start(bf16[160,1536]{1,0:T(8,128)(2,1)S(1)} %collective-permute-done.refs_1_) | copy-start | bytes 1474564
  87.1 6.0 %collective-permute-start.7 = (bf16[160,1536]{1,0:T(8,128)(2,1)S(1)}, bf16[160,1536]{1,0:T(8,128)(2,1)S(1)}, u32[]{:S(2)}, u32[]{:S(2)}) collective-permute-start(bf16[160,1536]{1,0:T(8,128)(2,1)S(1)} %collective-permute-done.refs_1_), channel_id=1, source_target_pairs={{0,1},{1,0},{2,3},{3,2},{4,5},{5,4},{6,7},{7,6},{8,9},{9,8},{10,11... | collective-permute-start | bytes 1474568 | tf_op jit(solution)/shard_map/ppermute | solution.py:484
  87.2 18.7 %collective-permute-start.4 = (bf16[160,2048]{1,0:T(8,128)(2,1)}, bf16[160,2048]{1,0:T(8,128)(2,1)}, u32[]{:S(2)}, u32[]{:S(2)}) collective-permute-start(bf16[160,2048]{1,0:T(8,128)(2,1)} %get-tuple-element.54), channel_id=1, source_target_pairs={{0,2},{1,3},{2,4},{3,5},{4,6},{5,7},{6,0},{7,1},{8,10},{9,11},{10,... | collective-permute-start | bytes 1966088 | tf_op jit(solution)/shard_map/ppermute | solution.py:480
  88.9 32.3 %collective-permute-start.5 = (bf16[160,2048]{1,0:T(8,128)(2,1)}, bf16[160,2048]{1,0:T(8,128)(2,1)}, u32[]{:S(2)}, u32[]{:S(2)}) collective-permute-start(bf16[160,2048]{1,0:T(8,128)(2,1)} %get-tuple-element.55), channel_id=1, source_target_pairs={{0,4},{1,5},{2,6},{3,7},{4,0},{5,1},{6,2},{7,3},{8,12},{9,13},{10,... | collective-permute-start | bytes 1966088 | tf_op jit(solution)/shard_map/ppermute | solution.py:480
  91.8 29.4 %collective-permute-start.6 = (bf16[160,2048]{1,0:T(8,128)(2,1)}, bf16[160,2048]{1,0:T(8,128)(2,1)}, u32[]{:S(2)}, u32[]{:S(2)}) collective-permute-start(bf16[160,2048]{1,0:T(8,128)(2,1)} %get-tuple-element.56), channel_id=1, source_target_pairs={{0,6},{1,7},{2,0},{3,1},{4,2},{5,3},{6,4},{7,5},{8,14},{9,15},{10,... | collective-permute-start | bytes 1966088 | tf_op jit(solution)/shard_map/ppermute | solution.py:480
  93.1 2.2 collective-permute-start.8
  93.9 2.3 collective-permute-start.9
  95.3 26.4 %collective-permute-start.10 = (bf16[160,2048]{1,0:T(8,128)(2,1)}, bf16[160,2048]{1,0:T(8,128)(2,1)}, u32[]{:S(2)}, u32[]{:S(2)}) collective-permute-start(bf16[160,2048]{1,0:T(8,128)(2,1)} %get-tuple-element.53.refs_0_), channel_id=1, source_target_pairs={{0,1},{1,0},{2,3},{3,2},{4,5},{5,4},{6,7},{7,6},{8,9},{9,8},{10,11... | collective-permute-start | bytes 1966088 | tf_op jit(solution)/shard_map/ppermute | solution.py:484
  121.2 3.2 %collective-permute-start.11 = (bf16[160,2048]{1,0:T(8,128)(2,1)}, bf16[160,2048]{1,0:T(8,128)(2,1)S(1)}, u32[]{:S(2)}, u32[]{:S(2)}) collective-permute-start(bf16[160,2048]{1,0:T(8,128)(2,1)} %collective-permute-done.4.refs_1_), channel_id=1, source_target_pairs={{0,1},{1,0},{2,3},{3,2},{4,5},{5,4},{6,7},{7,6},{8,9},{9,8},{10,11... | collective-permute-start | bytes 1966088 | tf_op jit(solution)/shard_map/ppermute | solution.py:484
  121.2 3.4 %collective-permute-start.12 = (bf16[160,2048]{1,0:T(8,128)(2,1)}, bf16[160,2048]{1,0:T(8,128)(2,1)}, u32[]{:S(2)}, u32[]{:S(2)}) collective-permute-start(bf16[160,2048]{1,0:T(8,128)(2,1)} %collective-permute-done.5.refs_2_), channel_id=1, source_target_pairs={{0,1},{1,0},{2,3},{3,2},{4,5},{5,4},{6,7},{7,6},{8,9},{9,8},{10,11... | collective-permute-start | bytes 1966088 | tf_op jit(solution)/shard_map/ppermute | solution.py:484
  121.7 3.8 %collective-permute-start.13 = (bf16[160,2048]{1,0:T(8,128)(2,1)}, bf16[160,2048]{1,0:T(8,128)(2,1)}, u32[]{:S(2)}, u32[]{:S(2)}) collective-permute-start(bf16[160,2048]{1,0:T(8,128)(2,1)} %collective-permute-done.6.refs_3_), channel_id=1, source_target_pairs={{0,1},{1,0},{2,3},{3,2},{4,5},{5,4},{6,7},{7,6},{8,9},{9,8},{10,11... | collective-permute-start | bytes 1966088 | tf_op jit(solution)/shard_map/ppermute | solution.py:484
  137.1 5.8 %collective-permute-start.18 = (bf16[640,1536]{1,0:T(8,128)(2,1)}, bf16[640,1536]{1,0:T(8,128)(2,1)}, u32[]{:S(2)}, u32[]{:S(2)}) collective-permute-start(bf16[640,1536]{1,0:T(8,128)(2,1)} %get-tuple-element.74), channel_id=1, source_target_pairs={{0,1},{1,0},{2,3},{3,2},{4,5},{5,4},{6,7},{7,6},{8,9},{9,8},{10,11... | collective-permute-start | bytes 5898248 | tf_op jit(solution)/shard_map/ppermute | solution.py:484
  142.4 8.3 %collective-permute-start.14 = (bf16[640,2048]{1,0:T(8,128)(2,1)}, bf16[640,2048]{1,0:T(8,128)(2,1)}, u32[]{:S(2)}, u32[]{:S(2)}) collective-permute-start(bf16[640,2048]{1,0:T(8,128)(2,1)} %down_other.1), channel_id=1, source_target_pairs={{0,1},{1,0},{2,3},{3,2},{4,5},{5,4},{6,7},{7,6},{8,9},{9,8},{10,11... | collective-permute-start | bytes 7864328 | tf_op jit(solution)/shard_map/ppermute | solution.py:484
  146.8 24.3 %collective-permute-start.19 = (bf16[160,1536]{1,0:T(8,128)(2,1)}, bf16[160,1536]{1,0:T(8,128)(2,1)S(1)}, u32[]{:S(2)}, u32[]{:S(2)}) collective-permute-start(bf16[160,1536]{1,0:T(8,128)(2,1)} %get-tuple-element.76), channel_id=1, source_target_pairs={{0,6},{1,7},{2,0},{3,1},{4,2},{5,3},{6,4},{7,5},{8,14},{9,15},{10,... | collective-permute-start | bytes 1474568 | tf_op jit(solution)/shard_map/ppermute | solution.py:480
  148.8 22.3 %collective-permute-start.20 = (bf16[160,1536]{1,0:T(8,128)(2,1)}, bf16[160,1536]{1,0:T(8,128)(2,1)S(1)}, u32[]{:S(2)}, u32[]{:S(2)}) collective-permute-start(bf16[160,1536]{1,0:T(8,128)(2,1)} %get-tuple-element.77), channel_id=1, source_target_pairs={{0,4},{1,5},{2,6},{3,7},{4,0},{5,1},{6,2},{7,3},{8,12},{9,13},{10,... | collective-permute-start | bytes 1474568 | tf_op jit(solution)/shard_map/ppermute | solution.py:480
  150.0 25.4 %collective-permute-start.21 = (bf16[160,1536]{1,0:T(8,128)(2,1)}, bf16[160,1536]{1,0:T(8,128)(2,1)}, u32[]{:S(2)}, u32[]{:S(2)}) collective-permute-start(bf16[160,1536]{1,0:T(8,128)(2,1)} %get-tuple-element.78), channel_id=1, source_target_pairs={{0,2},{1,3},{2,4},{3,5},{4,6},{5,7},{6,0},{7,1},{8,10},{9,11},{10,... | collective-permute-start | bytes 1474568 | tf_op jit(solution)/shard_map/ppermute | solution.py:480
  156.1 42.5 %collective-permute-start.15 = (bf16[160,2048]{1,0:T(8,128)(2,1)}, bf16[160,2048]{1,0:T(8,128)(2,1)}, u32[]{:S(2)}, u32[]{:S(2)}) collective-permute-start(bf16[160,2048]{1,0:T(8,128)(2,1)} %get-tuple-element.71), channel_id=1, source_target_pairs={{0,6},{1,7},{2,0},{3,1},{4,2},{5,3},{6,4},{7,5},{8,14},{9,15},{10,... | collective-permute-start | bytes 1966088 | tf_op jit(solution)/shard_map/ppermute | solution.py:480
  158.5 40.1 %collective-permute-start.16 = (bf16[160,2048]{1,0:T(8,128)(2,1)}, bf16[160,2048]{1,0:T(8,128)(2,1)}, u32[]{:S(2)}, u32[]{:S(2)}) collective-permute-start(bf16[160,2048]{1,0:T(8,128)(2,1)} %get-tuple-element.72), channel_id=1, source_target_pairs={{0,4},{1,5},{2,6},{3,7},{4,0},{5,1},{6,2},{7,3},{8,12},{9,13},{10,... | collective-permute-start | bytes 1966088 | tf_op jit(solution)/shard_map/ppermute | solution.py:480
  171.1 4.3 %copy-start.6 = (bf16[160,1536]{1,0:T(8,128)(2,1)}, bf16[160,1536]{1,0:T(8,128)(2,1)S(1)}, u32[]{:S(2)}) copy-start(bf16[160,1536]{1,0:T(8,128)(2,1)S(1)} %collective-permute-done.19.refs_1_) | copy-start | bytes 1474564
  171.1 31.1 %collective-permute-start.17 = (bf16[160,2048]{1,0:T(8,128)(2,1)}, bf16[160,2048]{1,0:T(8,128)(2,1)}, u32[]{:S(2)}, u32[]{:S(2)}) collective-permute-start(bf16[160,2048]{1,0:T(8,128)(2,1)} %get-tuple-element.73), channel_id=1, source_target_pairs={{0,2},{1,3},{2,4},{3,5},{4,6},{5,7},{6,0},{7,1},{8,10},{9,11},{10,... | collective-permute-start | bytes 1966088 | tf_op jit(solution)/shard_map/ppermute | solution.py:480
  171.1 4.3 %copy-start.7 = (bf16[160,1536]{1,0:T(8,128)(2,1)}, bf16[160,1536]{1,0:T(8,128)(2,1)S(1)}, u32[]{:S(2)}) copy-start(bf16[160,1536]{1,0:T(8,128)(2,1)S(1)} %collective-permute-done.20.refs_2_) | copy-start | bytes 1474564
  179.4 32.6 %all-to-all-start.3 = ((bf16[32,40,384]{2,1,0:T(8,128)(2,1)}), bf16[32,40,384]{2,1,0:T(8,128)(2,1)S(1)}, u32[]{:S(2)}, u32[]{:S(2)}) async-start(bf16[32,40,384]{2,1,0:T(8,128)(2,1)} %bitcast.16), calls=%async_computation.3 | async-start | bytes 1966080 | tf_op jit(solution)/shard_map/all_to_all | solution.py:475
  206.9 10.2 %copy-start.4 = (s32[128,4]{0,1:T(4,128)S(1)}, s32[128,4]{0,1:T(4,128)}, u32[]{:S(2)}) copy-start(s32[128,4]{0,1:T(4,128)} %param.7) | copy-start | bytes 6148
  211.9 5.9 %copy-start = (bf16[32,40,384]{2,1,0:T(8,128)(2,1)}, bf16[32,40,384]{2,1,0:T(8,128)(2,1)S(1)}, u32[]{:S(2)}) copy-start(bf16[32,40,384]{2,1,0:T(8,128)(2,1)S(1)} %all-to-all-done.3) | copy-start | bytes 2949124
  211.9 38.6 %all-to-all-start.2 = ((bf16[32,40,512]{2,1,0:T(8,128)(2,1)}), bf16[32,40,512]{2,1,0:T(8,128)(2,1)}, u32[]{:S(2)}, u32[]{:S(2)}) async-start(bf16[32,40,512]{2,1,0:T(8,128)(2,1)} %bitcast.13), calls=%async_computation.2 | async-start | bytes 2621440 | tf_op jit(solution)/shard_map/all_to_all | solution.py:475
  (2 other events, 1.9 us)

commit v2 on v1

--- a/solution.py
+++ b/solution.py
@@ -510,6 +510,7 @@
     values = down_own(hidden, w_down, mate, HOME[0])
     back = [values[0]] + [along_y(values[d], -d) for d in range(1, EXPERTS)]
     values = down_own(hidden, w_down, later_mate, HOME[1])
+    back[1], values = lax.optimization_barrier((back[1], values))
     later_back = [values[0]] + [along_y(values[d], -d) for d in range(1, EXPERTS)]
     home = over_nodes(mix(where, meta, back, nodes, HOME[0]), nodes)
     later_home = over_nodes(mix(where, meta, later_back, nodes, HOME[1]), nodes)

time: 256 us -> 256 us (level)
  no operation moved by 1% of the time
where the time goes in v2:
time: 256 us; the launch traced here: 255 us
  waiting for transfers between devices  135 us (53%)
  Pallas kernels  66.9 us (26%)
  starting transfers between devices  49.4 us (19%)
    all_to_all x4, waiting for transfers between devices, over_nodes(): lax.all_to_all(cut, 'node', split_axis=0, concat_axis=0, tiled=True)  82.4 us
    ppermute x12, waiting for transfers between devices, along_y(): return lax.ppermute(block, 'local', pairs)  47.4 us
    all_to_all x4, starting transfers between devices, over_nodes(): lax.all_to_all(cut, 'node', split_axis=0, concat_axis=0, tiled=True)  27.1 us
    ppermute x12, starting transfers between devices, along_y(): return lax.ppermute(block, 'local', pairs)  20.5 us
    pallas_call x1, Pallas kernels, hidden_step(): call(functools.partial(up_kernel, chunk.start, down_chunk.start), [jax.Sh...  11.5 us
    pallas_call x2, Pallas kernels, down_own(): call(down_own_kernel, [jax.ShapeDtypeStruct((part, span), BF)] * EXPERTS,...  9.19 us
    pallas_call x1, Pallas kernels, up_step(): call(functools.partial(up_kernel, chunk.start, None), [jax.ShapeDtypeStru...  8.75 us
    pallas_call x2, Pallas kernels, mix(): call(functools.partial(mix_kernel, chunk), jax.ShapeDtypeStruct((nodes *...  8.65 us
  transfers between devices with their start and end apart: 26, of which 15 were waited for; matrix products, arithmetic and copies ran while one was open for 1% of the time, Pallas kernels for 18%

profile of v2, /device:TPU:32, one launch (start us, length us, event | category | flops | bytes accessed | tf_op | source)
XLA Modules:
  0.0 254.7 jit_solution(12427759617999946012)
XLA Ops:
  0.0 4.1 %pack_rows.3 = bf16[1024,512]{1,0:T(8,128)(2,1)} custom-call(s32[4,128]{1,0:T(4,128)} %bitcast.17, bf16[4,128]{1,0:T(4,128)(2,1)} %bitcast.19, bf16[128,3584]{1,0:T(8,128)(2,1)} %tok_ref.3), custom_call_target="tpu_custom_call" | custom-call | flops 5000000000 | bytes 1000000 | tf_op jit(solution)/shard_map/pack_rows/pallas_call | solution.py:145
  4.1 11.2 %all-to-all-start = ((bf16[32,32,512]{2,1,0:T(8,128)(2,1)}), bf16[32,32,512]{2,1,0:T(8,128)(2,1)}, u32[]{:S(2)}, u32[]{:S(2)}) async-start(bf16[32,32,512]{2,1,0:T(8,128)(2,1)} %bitcast.14), calls=%async_computation | async-start | bytes 2097152 | tf_op jit(solution)/shard_map/all_to_all | solution.py:475
  16.0 3.3 %pack_rows.2 = bf16[1280,512]{1,0:T(8,128)(2,1)} custom-call(s32[4,128]{1,0:T(4,128)} %bitcast.18, bf16[4,128]{1,0:T(4,128)(2,1)} %bitcast.20, bf16[128,3584]{1,0:T(8,128)(2,1)} %tok_ref.3), custom_call_target="tpu_custom_call" | custom-call | flops 5000000000 | bytes 1000000 | tf_op jit(solution)/shard_map/pack_rows/pallas_call | solution.py:145
  19.3 24.6 %all-to-all-done = bf16[32,32,512]{2,1,0:T(8,128)(2,1)} async-done(((bf16[32,32,512]{2,1,0:T(8,128)(2,1)}), bf16[32,32,512]{2,1,0:T(8,128)(2,1)}, u32[]{:S(2)}, u32[]{:S(2)}) %all-to-all-start) | async-done | bytes 1048608 | tf_op jit(solution)/shard_map/all_to_all | solution.py:475
  43.9 5.2 %all-to-all-start.1 = ((bf16[32,40,512]{2,1,0:T(8,128)(2,1)}), bf16[32,40,512]{2,1,0:T(8,128)(2,1)}, u32[]{:S(2)}, u32[]{:S(2)}) async-start(bf16[32,40,512]{2,1,0:T(8,128)(2,1)} %bitcast.12), calls=%async_computation.1 | async-start | bytes 2621440 | tf_op jit(solution)/shard_map/all_to_all | solution.py:475
  49.2 3.6 %select_rows.2 = (f32[32,256]{1,0:T(8,128)}, bf16[160,1536]{1,0:T(8,128)(2,1)}, bf16[160,1536]{1,0:T(8,128)(2,1)}, bf16[160,1536]{1,0:T(8,128)(2,1)}, bf16[160,1536]{1,0:T(8,128)(2,1)}) custom-call(s32[2]{0:T(128)} %pad_add_fusion.where_ref, bf16[1024,512]{1,0:T(8,128)(2,1)} %bitcast.5.rows_ref), custom_call_target="tpu_custom_call" | custom-call | flops 20000000000 | bytes 1000000 | tf_op jit(solution)/shard_map/select_rows/pallas_call | solution.py:225
  52.8 1.6 collective-permute-start
  54.4 2.9 %collective-permute-start.1 = (bf16[160,1536]{1,0:T(8,128)(2,1)}, bf16[160,1536]{1,0:T(8,128)(2,1)}, u32[]{:S(2)}, u32[]{:S(2)}) collective-permute-start(bf16[160,1536]{1,0:T(8,128)(2,1)} %get-tuple-element.51), channel_id=1, source_target_pairs={{0,4},{1,5},{2,6},{3,7},{4,0},{5,1},{6,2},{7,3},{8,12},{9,13},{10,... | collective-permute-start | bytes 1474568 | tf_op jit(solution)/shard_map/ppermute | solution.py:480
  58.6 24.0 %all-to-all-done.1 = bf16[32,40,512]{2,1,0:T(8,128)(2,1)} async-done(((bf16[32,40,512]{2,1,0:T(8,128)(2,1)}), bf16[32,40,512]{2,1,0:T(8,128)(2,1)}, u32[]{:S(2)}, u32[]{:S(2)}) %all-to-all-start.1) | async-done | bytes 1310752 | tf_op jit(solution)/shard_map/all_to_all | solution.py:475
  82.6 4.5 %select_rows.3 = (bf16[160,2048]{1,0:T(8,128)(2,1)}, bf16[160,2048]{1,0:T(8,128)(2,1)}, bf16[160,2048]{1,0:T(8,128)(2,1)}, bf16[160,2048]{1,0:T(8,128)(2,1)}) custom-call(s32[2]{0:T(128)} %pad_add_fusion.where_ref, bf16[1280,512]{1,0:T(8,128)(2,1)} %bitcast.7.rows_ref, f32[32,256]{1,0:T(8,128)} %get-tuple-element.48.out_refs_0_.meta_ref), custom_call_target="tpu_custom_call" | custom-call | flops 20000000000 | bytes 1000000 | tf_op jit(solution)/shard_map/select_rows/pallas_call | solution.py:225
  87.2 1.7 collective-permute-start.4
  88.9 2.9 %collective-permute-start.5 = (bf16[160,2048]{1,0:T(8,128)(2,1)}, bf16[160,2048]{1,0:T(8,128)(2,1)}, u32[]{:S(2)}, u32[]{:S(2)}) collective-permute-start(bf16[160,2048]{1,0:T(8,128)(2,1)} %get-tuple-element.60), channel_id=1, source_target_pairs={{0,4},{1,5},{2,6},{3,7},{4,0},{5,1},{6,2},{7,3},{8,12},{9,13},{10,... | collective-permute-start | bytes 1966088 | tf_op jit(solution)/shard_map/ppermute | solution.py:480
  96.3 8.7 %gate_up.1 = (f32[1280,512]{1,0:T(8,128)}, f32[1280,512]{1,0:T(8,128)}) custom-call(bf16[160,1536]{1,0:T(8,128)(2,1)} %get-tuple-element.62.refs_0_, bf16[160,1536]{1,0:T(8,128)(2,1)} %copy-done.2, bf16[160,1536]{1,0:T(8,128)(2,1)} %collective-permute-done.1.refs_2_, bf16[160,1536]{1,0:T(8,128)(2,1)} %collective-permute-done.2.refs_3_, ...), custom_call_target="tpu_custom_call" | custom-call | flops 1000000000 | bytes 1000000 | tf_op jit(solution)/shard_map/gate_up/pallas_call | solution.py:382
  106.0 15.2 %collective-permute-done.5.refs_2_ = bf16[160,2048]{1,0:T(8,128)(2,1)} collective-permute-done((bf16[160,2048]{1,0:T(8,128)(2,1)}, bf16[160,2048]{1,0:T(8,128)(2,1)}, u32[]{:S(2)}, u32[]{:S(2)}) %collective-permute-start.5) | collective-permute-done | bytes 655392 | tf_op jit(solution)/shard_map/ppermute | solution.py:480
  121.7 2.7 %collective-permute-done.11.refs_5_ = bf16[160,2048]{1,0:T(8,128)(2,1)S(1)} collective-permute-done((bf16[160,2048]{1,0:T(8,128)(2,1)}, bf16[160,2048]{1,0:T(8,128)(2,1)S(1)}, u32[]{:S(2)}, u32[]{:S(2)}) %collective-permute-start.11) | collective-permute-done | bytes 655392 | tf_op jit(solution)/shard_map/ppermute | solution.py:484
  125.5 11.5 %hidden_down.1 = (bf16[1280,512]{1,0:T(8,128)(2,1)}, bf16[640,1536]{1,0:T(8,128)(2,1)}) custom-call(bf16[160,2048]{1,0:T(8,128)(2,1)} %get-tuple-element.58.refs_0_, bf16[160,2048]{1,0:T(8,128)(2,1)} %collective-permute-done.4.refs_1_, bf16[160,2048]{1,0:T(8,128)(2,1)} %collective-permute-done.5.refs_2_, bf16[160,2048]{1,0:T(8,128)(2,1)} %collective-permute-done.6.refs_3_, ...), custom_call_target="tpu_custom_call" | custom-call | flops 10000000000 | bytes 1000000 | tf_op jit(solution)/shard_map/hidden_down/pallas_call | solution.py:403
  137.3 5.2 %down_other.1 = bf16[640,2048]{1,0:T(8,128)(2,1)} custom-call(bf16[1280,512]{1,0:T(8,128)(2,1)} %get-tuple-element.74.hidden_ref, bf16[1,512,3584]{2,1,0:T(8,128)(2,1)} %w_ref.5), custom_call_target="tpu_custom_call" | custom-call | flops 4000000000 | bytes 1000000 | tf_op jit(solution)/shard_map/down_other/pallas_call | solution.py:439
  142.8 3.9 %down_own.2 = (bf16[160,1536]{1,0:T(8,128)(2,1)}, bf16[160,1536]{1,0:T(8,128)(2,1)}, bf16[160,1536]{1,0:T(8,128)(2,1)}, bf16[160,1536]{1,0:T(8,128)(2,1)}) custom-call(bf16[1280,512]{1,0:T(8,128)(2,1)} %get-tuple-element.74.hidden_ref, bf16[1,512,3584]{2,1,0:T(8,128)(2,1)} %w_ref.5, bf16[640,1536]{1,0:T(8,128)(2,1)} %collective-permute-done.14.mate_ref), custom_call_target="tpu_custom_call" | custom-call | flops 10000000000 | bytes 1000000 | tf_op jit(solution)/shard_map/down_own/pallas_call | solution.py:458
  146.7 2.1 collective-permute-start.15
  150.7 5.3 %down_own.3 = (bf16[160,2048]{1,0:T(8,128)(2,1)}, bf16[160,2048]{1,0:T(8,128)(2,1)}, bf16[160,2048]{1,0:T(8,128)(2,1)}, bf16[160,2048]{1,0:T(8,128)(2,1)}) custom-call(bf16[1280,512]{1,0:T(8,128)(2,1)} %get-tuple-element.74.hidden_ref, bf16[1,512,3584]{2,1,0:T(8,128)(2,1)} %w_ref.5, bf16[640,2048]{1,0:T(8,128)(2,1)} %collective-permute-done.16.mate_ref), custom_call_target="tpu_custom_call" | custom-call | flops 4000000000 | bytes 1000000 | tf_op jit(solution)/shard_map/down_own/pallas_call | solution.py:458
  156.0 14.5 %collective-permute-done.15.refs_1_ = bf16[160,1536]{1,0:T(8,128)(2,1)S(1)} collective-permute-done((bf16[160,1536]{1,0:T(8,128)(2,1)}, bf16[160,1536]{1,0:T(8,128)(2,1)S(1)}, u32[]{:S(2)}, u32[]{:S(2)}) %collective-permute-start.15) | collective-permute-done | bytes 491552 | tf_op jit(solution)/shard_map/ppermute | solution.py:480
  170.5 3.9 %collective-permute-start.17 = (bf16[160,2048]{1,0:T(8,128)(2,1)}, bf16[160,2048]{1,0:T(8,128)(2,1)}, u32[]{:S(2)}, u32[]{:S(2)}) collective-permute-start(bf16[160,2048]{1,0:T(8,128)(2,1)} %get-tuple-element.82), channel_id=1, source_target_pairs={{0,6},{1,7},{2,0},{3,1},{4,2},{5,3},{6,4},{7,5},{8,14},{9,15},{10,... | collective-permute-start | bytes 1966088 | tf_op jit(solution)/shard_map/ppermute | solution.py:480
  176.1 4.0 %node_share.3 = bf16[1280,384]{1,0:T(8,128)(2,1)} custom-call(s32[2]{0:T(128)} %pad_add_fusion.where_ref, f32[32,256]{1,0:T(8,128)} %get-tuple-element.48.out_refs_0_.meta_ref, bf16[160,1536]{1,0:T(8,128)(2,1)} %get-tuple-element.85.refs_0_, bf16[160,1536]{1,0:T(8,128)(2,1)} %copy-done.6, bf16[160,1536]{1,0:T(8,128)(2,1)} %copy-done.7, ...), custom_call_target="tpu_custom_call" | custom-call | flops 40000000000 | bytes 1000000 | tf_op jit(solution)/shard_map/node_share/pallas_call | solution.py:274
  180.1 5.5 %all-to-all-start.3 = ((bf16[32,40,384]{2,1,0:T(8,128)(2,1)}), bf16[32,40,384]{2,1,0:T(8,128)(2,1)S(1)}, u32[]{:S(2)}, u32[]{:S(2)}) async-start(bf16[32,40,384]{2,1,0:T(8,128)(2,1)} %bitcast.16), calls=%async_computation.3 | async-start | bytes 1966080 | tf_op jit(solution)/shard_map/all_to_all | solution.py:475
  185.5 13.0 %collective-permute-done.17.refs_1_ = bf16[160,2048]{1,0:T(8,128)(2,1)} collective-permute-done((bf16[160,2048]{1,0:T(8,128)(2,1)}, bf16[160,2048]{1,0:T(8,128)(2,1)}, u32[]{:S(2)}, u32[]{:S(2)}) %collective-permute-start.17) | collective-permute-done | bytes 655392 | tf_op jit(solution)/shard_map/ppermute | solution.py:480
  198.6 3.7 %collective-permute-done.19.refs_3_ = bf16[160,2048]{1,0:T(8,128)(2,1)} collective-permute-done((bf16[160,2048]{1,0:T(8,128)(2,1)}, bf16[160,2048]{1,0:T(8,128)(2,1)}, u32[]{:S(2)}, u32[]{:S(2)}) %collective-permute-start.19) | collective-permute-done | bytes 655392 | tf_op jit(solution)/shard_map/ppermute | solution.py:480
  202.2 4.7 %node_share.2 = bf16[1280,512]{1,0:T(8,128)(2,1)} custom-call(s32[2]{0:T(128)} %pad_add_fusion.where_ref, f32[32,256]{1,0:T(8,128)} %get-tuple-element.48.out_refs_0_.meta_ref, bf16[160,2048]{1,0:T(8,128)(2,1)} %get-tuple-element.81.refs_0_, bf16[160,2048]{1,0:T(8,128)(2,1)} %collective-permute-done.17.refs_1_, ...), custom_call_target="tpu_custom_call" | custom-call | flops 40000000000 | bytes 1000000 | tf_op jit(solution)/shard_map/node_share/pallas_call | solution.py:274
  206.9 5.1 %all-to-all-done.3 = bf16[32,40,384]{2,1,0:T(8,128)(2,1)S(1)} async-done(((bf16[32,40,384]{2,1,0:T(8,128)(2,1)}), bf16[32,40,384]{2,1,0:T(8,128)(2,1)S(1)}, u32[]{:S(2)}, u32[]{:S(2)}) %all-to-all-start.3) | async-done | bytes 983072 | tf_op jit(solution)/shard_map/all_to_all | solution.py:475
  212.0 5.1 %all-to-all-start.2 = ((bf16[32,40,512]{2,1,0:T(8,128)(2,1)}), bf16[32,40,512]{2,1,0:T(8,128)(2,1)}, u32[]{:S(2)}, u32[]{:S(2)}) async-start(bf16[32,40,512]{2,1,0:T(8,128)(2,1)} %bitcast.13), calls=%async_computation.2 | async-start | bytes 2621440 | tf_op jit(solution)/shard_map/all_to_all | solution.py:475
  217.8 3.8 %sum_over_nodes.2.refs_0_ = bf16[128,1536]{1,0:T(8,128)(2,1)} custom-call(s32[128,4]{1,0:T(8,128)} %copy.8.ids_ref, bf16[1280,384]{1,0:T(8,128)(2,1)} %bitcast.15), custom_call_target="tpu_custom_call" | custom-call | flops 6000000000 | bytes 1000000 | tf_op jit(solution)/shard_map/sum_over_nodes/pallas_call | solution.py:317
  221.7 28.7 %all-to-all-done.2 = bf16[32,40,512]{2,1,0:T(8,128)(2,1)} async-done(((bf16[32,40,512]{2,1,0:T(8,128)(2,1)}), bf16[32,40,512]{2,1,0:T(8,128)(2,1)}, u32[]{:S(2)}, u32[]{:S(2)}) %all-to-all-start.2) | async-done | bytes 1310752 | tf_op jit(solution)/shard_map/all_to_all | solution.py:475
  250.4 4.3 %sum_over_nodes.3 = bf16[128,3584]{1,0:T(8,128)(2,1)} custom-call(s32[128,4]{1,0:T(8,128)} %copy.8.ids_ref, bf16[1280,512]{1,0:T(8,128)(2,1)} %bitcast.9.home_ref, bf16[128,1536]{1,0:T(8,128)(2,1)} %sum_over_nodes.2.refs_0_), custom_call_target="tpu_custom_call" | custom-call | flops 6000000000 | bytes 1000000 | tf_op jit(solution)/shard_map/sum_over_nodes/pallas_call | solution.py:317
  (51 shorter events, 14.1 us)
Async XLA Ops:
  4.1 39.8 %all-to-all-start = ((bf16[32,32,512]{2,1,0:T(8,128)(2,1)}), bf16[32,32,512]{2,1,0:T(8,128)(2,1)}, u32[]{:S(2)}, u32[]{:S(2)}) async-start(bf16[32,32,512]{2,1,0:T(8,128)(2,1)} %bitcast.14), calls=%async_computation | async-start | bytes 2097152 | tf_op jit(solution)/shard_map/all_to_all | solution.py:475
  43.9 38.7 %all-to-all-start.1 = ((bf16[32,40,512]{2,1,0:T(8,128)(2,1)}), bf16[32,40,512]{2,1,0:T(8,128)(2,1)}, u32[]{:S(2)}, u32[]{:S(2)}) async-start(bf16[32,40,512]{2,1,0:T(8,128)(2,1)} %bitcast.12), calls=%async_computation.1 | async-start | bytes 2621440 | tf_op jit(solution)/shard_map/all_to_all | solution.py:475
  52.8 34.3 %collective-permute-start.3 = (bf16[160,1536]{1,0:T(8,128)(2,1)}, bf16[160,1536]{1,0:T(8,128)(2,1)S(1)}, u32[]{:S(2)}, u32[]{:S(2)}) collective-permute-start(bf16[160,1536]{1,0:T(8,128)(2,1)} %get-tuple-element.62.refs_0_), channel_id=1, source_target_pairs={{0,1},{1,0},{2,3},{3,2},{4,5},{5,4},{6,7},{7,6},{8,9},{9,8},{10,11... | collective-permute-start | bytes 1474568 | tf_op jit(solution)/shard_map/ppermute | solution.py:484
  52.8 34.3 %collective-permute-start = (bf16[160,1536]{1,0:T(8,128)(2,1)}, bf16[160,1536]{1,0:T(8,128)(2,1)S(1)}, u32[]{:S(2)}, u32[]{:S(2)}) collective-permute-start(bf16[160,1536]{1,0:T(8,128)(2,1)} %get-tuple-element.50), channel_id=1, source_target_pairs={{0,2},{1,3},{2,4},{3,5},{4,6},{5,7},{6,0},{7,1},{8,10},{9,11},{10,... | collective-permute-start | bytes 1474568 | tf_op jit(solution)/shard_map/ppermute | solution.py:480
  54.4 32.7 %collective-permute-start.1 = (bf16[160,1536]{1,0:T(8,128)(2,1)}, bf16[160,1536]{1,0:T(8,128)(2,1)}, u32[]{:S(2)}, u32[]{:S(2)}) collective-permute-start(bf16[160,1536]{1,0:T(8,128)(2,1)} %get-tuple-element.51), channel_id=1, source_target_pairs={{0,4},{1,5},{2,6},{3,7},{4,0},{5,1},{6,2},{7,3},{8,12},{9,13},{10,... | collective-permute-start | bytes 1474568 | tf_op jit(solution)/shard_map/ppermute | solution.py:480
  57.3 29.9 %collective-permute-start.2 = (bf16[160,1536]{1,0:T(8,128)(2,1)}, bf16[160,1536]{1,0:T(8,128)(2,1)}, u32[]{:S(2)}, u32[]{:S(2)}) collective-permute-start(bf16[160,1536]{1,0:T(8,128)(2,1)} %get-tuple-element.52), channel_id=1, source_target_pairs={{0,6},{1,7},{2,0},{3,1},{4,2},{5,3},{6,4},{7,5},{8,14},{9,15},{10,... | collective-permute-start | bytes 1474568 | tf_op jit(solution)/shard_map/ppermute | solution.py:480
  87.1 9.2 %copy-start.1 = (bf16[160,1536]{1,0:T(8,128)(2,1)}, bf16[160,1536]{1,0:T(8,128)(2,1)S(1)}, u32[]{:S(2)}) copy-start(bf16[160,1536]{1,0:T(8,128)(2,1)S(1)} %collective-permute-done.3.refs_4_) | copy-start | bytes 1474564
  87.1 9.2 %copy-start.2 = (bf16[160,1536]{1,0:T(8,128)(2,1)}, bf16[160,1536]{1,0:T(8,128)(2,1)S(1)}, u32[]{:S(2)}) copy-start(bf16[160,1536]{1,0:T(8,128)(2,1)S(1)} %collective-permute-done.refs_1_) | copy-start | bytes 1474564
  87.1 6.0 %collective-permute-start.7 = (bf16[160,1536]{1,0:T(8,128)(2,1)S(1)}, bf16[160,1536]{1,0:T(8,128)(2,1)S(1)}, u32[]{:S(2)}, u32[]{:S(2)}) collective-permute-start(bf16[160,1536]{1,0:T(8,128)(2,1)S(1)} %collective-permute-done.refs_1_), channel_id=1, source_target_pairs={{0,1},{1,0},{2,3},{3,2},{4,5},{5,4},{6,7},{7,6},{8,9},{9,8},{10,11... | collective-permute-start | bytes 1474568 | tf_op jit(solution)/shard_map/ppermute | solution.py:484
  87.2 18.7 %collective-permute-start.4 = (bf16[160,2048]{1,0:T(8,128)(2,1)}, bf16[160,2048]{1,0:T(8,128)(2,1)}, u32[]{:S(2)}, u32[]{:S(2)}) collective-permute-start(bf16[160,2048]{1,0:T(8,128)(2,1)} %get-tuple-element.59), channel_id=1, source_target_pairs={{0,2},{1,3},{2,4},{3,5},{4,6},{5,7},{6,0},{7,1},{8,10},{9,11},{10,... | collective-permute-start | bytes 1966088 | tf_op jit(solution)/shard_map/ppermute | solution.py:480
  88.9 32.3 %collective-permute-start.5 = (bf16[160,2048]{1,0:T(8,128)(2,1)}, bf16[160,2048]{1,0:T(8,128)(2,1)}, u32[]{:S(2)}, u32[]{:S(2)}) collective-permute-start(bf16[160,2048]{1,0:T(8,128)(2,1)} %get-tuple-element.60), channel_id=1, source_target_pairs={{0,4},{1,5},{2,6},{3,7},{4,0},{5,1},{6,2},{7,3},{8,12},{9,13},{10,... | collective-permute-start | bytes 1966088 | tf_op jit(solution)/shard_map/ppermute | solution.py:480
  91.8 29.4 %collective-permute-start.6 = (bf16[160,2048]{1,0:T(8,128)(2,1)}, bf16[160,2048]{1,0:T(8,128)(2,1)}, u32[]{:S(2)}, u32[]{:S(2)}) collective-permute-start(bf16[160,2048]{1,0:T(8,128)(2,1)} %get-tuple-element.61), channel_id=1, source_target_pairs={{0,6},{1,7},{2,0},{3,1},{4,2},{5,3},{6,4},{7,5},{8,14},{9,15},{10,... | collective-permute-start | bytes 1966088 | tf_op jit(solution)/shard_map/ppermute | solution.py:480
  93.1 2.2 collective-permute-start.8
  93.9 2.3 collective-permute-start.9
  95.3 26.4 %collective-permute-start.10 = (bf16[160,2048]{1,0:T(8,128)(2,1)}, bf16[160,2048]{1,0:T(8,128)(2,1)}, u32[]{:S(2)}, u32[]{:S(2)}) collective-permute-start(bf16[160,2048]{1,0:T(8,128)(2,1)} %get-tuple-element.58.refs_0_), channel_id=1, source_target_pairs={{0,1},{1,0},{2,3},{3,2},{4,5},{5,4},{6,7},{7,6},{8,9},{9,8},{10,11... | collective-permute-start | bytes 1966088 | tf_op jit(solution)/shard_map/ppermute | solution.py:484
  121.2 3.2 %collective-permute-start.11 = (bf16[160,2048]{1,0:T(8,128)(2,1)}, bf16[160,2048]{1,0:T(8,128)(2,1)S(1)}, u32[]{:S(2)}, u32[]{:S(2)}) collective-permute-start(bf16[160,2048]{1,0:T(8,128)(2,1)} %collective-permute-done.4.refs_1_), channel_id=1, source_target_pairs={{0,1},{1,0},{2,3},{3,2},{4,5},{5,4},{6,7},{7,6},{8,9},{9,8},{10,11... | collective-permute-start | bytes 1966088 | tf_op jit(solution)/shard_map/ppermute | solution.py:484
  121.2 3.4 %collective-permute-start.12 = (bf16[160,2048]{1,0:T(8,128)(2,1)}, bf16[160,2048]{1,0:T(8,128)(2,1)}, u32[]{:S(2)}, u32[]{:S(2)}) collective-permute-start(bf16[160,2048]{1,0:T(8,128)(2,1)} %collective-permute-done.5.refs_2_), channel_id=1, source_target_pairs={{0,1},{1,0},{2,3},{3,2},{4,5},{5,4},{6,7},{7,6},{8,9},{9,8},{10,11... | collective-permute-start | bytes 1966088 | tf_op jit(solution)/shard_map/ppermute | solution.py:484
  121.7 3.8 %collective-permute-start.13 = (bf16[160,2048]{1,0:T(8,128)(2,1)}, bf16[160,2048]{1,0:T(8,128)(2,1)}, u32[]{:S(2)}, u32[]{:S(2)}) collective-permute-start(bf16[160,2048]{1,0:T(8,128)(2,1)} %collective-permute-done.6.refs_3_), channel_id=1, source_target_pairs={{0,1},{1,0},{2,3},{3,2},{4,5},{5,4},{6,7},{7,6},{8,9},{9,8},{10,11... | collective-permute-start | bytes 1966088 | tf_op jit(solution)/shard_map/ppermute | solution.py:484
  124.4 1.1 copy-start.5
  137.1 5.8 %collective-permute-start.14 = (bf16[640,1536]{1,0:T(8,128)(2,1)}, bf16[640,1536]{1,0:T(8,128)(2,1)}, u32[]{:S(2)}, u32[]{:S(2)}) collective-permute-start(bf16[640,1536]{1,0:T(8,128)(2,1)} %get-tuple-element.75), channel_id=1, source_target_pairs={{0,1},{1,0},{2,3},{3,2},{4,5},{5,4},{6,7},{7,6},{8,9},{9,8},{10,11... | collective-permute-start | bytes 5898248 | tf_op jit(solution)/shard_map/ppermute | solution.py:484
  142.4 8.3 %collective-permute-start.16 = (bf16[640,2048]{1,0:T(8,128)(2,1)}, bf16[640,2048]{1,0:T(8,128)(2,1)}, u32[]{:S(2)}, u32[]{:S(2)}) collective-permute-start(bf16[640,2048]{1,0:T(8,128)(2,1)} %down_other.1), channel_id=1, source_target_pairs={{0,1},{1,0},{2,3},{3,2},{4,5},{5,4},{6,7},{7,6},{8,9},{9,8},{10,11... | collective-permute-start | bytes 7864328 | tf_op jit(solution)/shard_map/ppermute | solution.py:484
  146.7 23.8 %collective-permute-start.15 = (bf16[160,1536]{1,0:T(8,128)(2,1)}, bf16[160,1536]{1,0:T(8,128)(2,1)S(1)}, u32[]{:S(2)}, u32[]{:S(2)}) collective-permute-start(bf16[160,1536]{1,0:T(8,128)(2,1)} %get-tuple-element.76), channel_id=1, source_target_pairs={{0,6},{1,7},{2,0},{3,1},{4,2},{5,3},{6,4},{7,5},{8,14},{9,15},{10,... | collective-permute-start | bytes 1474568 | tf_op jit(solution)/shard_map/ppermute | solution.py:480
  148.8 26.5 %collective-permute-start.20 = (bf16[160,1536]{1,0:T(8,128)(2,1)}, bf16[160,1536]{1,0:T(8,128)(2,1)S(1)}, u32[]{:S(2)}, u32[]{:S(2)}) collective-permute-start(bf16[160,1536]{1,0:T(8,128)(2,1)} %get-tuple-element.87), channel_id=1, source_target_pairs={{0,4},{1,5},{2,6},{3,7},{4,0},{5,1},{6,2},{7,3},{8,12},{9,13},{10,... | collective-permute-start | bytes 1474568 | tf_op jit(solution)/shard_map/ppermute | solution.py:480
  149.9 25.4 %collective-permute-start.21 = (bf16[160,1536]{1,0:T(8,128)(2,1)}, bf16[160,1536]{1,0:T(8,128)(2,1)}, u32[]{:S(2)}, u32[]{:S(2)}) collective-permute-start(bf16[160,1536]{1,0:T(8,128)(2,1)} %get-tuple-element.88), channel_id=1, source_target_pairs={{0,2},{1,3},{2,4},{3,5},{4,6},{5,7},{6,0},{7,1},{8,10},{9,11},{10,... | collective-permute-start | bytes 1474568 | tf_op jit(solution)/shard_map/ppermute | solution.py:480
  170.5 4.9 %copy-start.6 = (bf16[160,1536]{1,0:T(8,128)(2,1)}, bf16[160,1536]{1,0:T(8,128)(2,1)S(1)}, u32[]{:S(2)}) copy-start(bf16[160,1536]{1,0:T(8,128)(2,1)S(1)} %collective-permute-done.15.refs_1_) | copy-start | bytes 1474564
  170.5 28.0 %collective-permute-start.17 = (bf16[160,2048]{1,0:T(8,128)(2,1)}, bf16[160,2048]{1,0:T(8,128)(2,1)}, u32[]{:S(2)}, u32[]{:S(2)}) collective-permute-start(bf16[160,2048]{1,0:T(8,128)(2,1)} %get-tuple-element.82), channel_id=1, source_target_pairs={{0,6},{1,7},{2,0},{3,1},{4,2},{5,3},{6,4},{7,5},{8,14},{9,15},{10,... | collective-permute-start | bytes 1966088 | tf_op jit(solution)/shard_map/ppermute | solution.py:480
  174.4 24.1 %collective-permute-start.18 = (bf16[160,2048]{1,0:T(8,128)(2,1)}, bf16[160,2048]{1,0:T(8,128)(2,1)}, u32[]{:S(2)}, u32[]{:S(2)}) collective-permute-start(bf16[160,2048]{1,0:T(8,128)(2,1)} %get-tuple-element.83), channel_id=1, source_target_pairs={{0,4},{1,5},{2,6},{3,7},{4,0},{5,1},{6,2},{7,3},{8,12},{9,13},{10,... | collective-permute-start | bytes 1966088 | tf_op jit(solution)/shard_map/ppermute | solution.py:480
  174.4 27.8 %collective-permute-start.19 = (bf16[160,2048]{1,0:T(8,128)(2,1)}, bf16[160,2048]{1,0:T(8,128)(2,1)}, u32[]{:S(2)}, u32[]{:S(2)}) collective-permute-start(bf16[160,2048]{1,0:T(8,128)(2,1)} %get-tuple-element.84), channel_id=1, source_target_pairs={{0,2},{1,3},{2,4},{3,5},{4,6},{5,7},{6,0},{7,1},{8,10},{9,11},{10,... | collective-permute-start | bytes 1966088 | tf_op jit(solution)/shard_map/ppermute | solution.py:480
  180.1 31.9 %all-to-all-start.3 = ((bf16[32,40,384]{2,1,0:T(8,128)(2,1)}), bf16[32,40,384]{2,1,0:T(8,128)(2,1)S(1)}, u32[]{:S(2)}, u32[]{:S(2)}) async-start(bf16[32,40,384]{2,1,0:T(8,128)(2,1)} %bitcast.16), calls=%async_computation.3 | async-start | bytes 1966080 | tf_op jit(solution)/shard_map/all_to_all | solution.py:475
  206.9 10.2 %copy-start.4 = (s32[128,4]{0,1:T(4,128)S(1)}, s32[128,4]{0,1:T(4,128)}, u32[]{:S(2)}) copy-start(s32[128,4]{0,1:T(4,128)} %param.7) | copy-start | bytes 6148
  212.0 5.9 %copy-start = (bf16[32,40,384]{2,1,0:T(8,128)(2,1)}, bf16[32,40,384]{2,1,0:T(8,128)(2,1)S(1)}, u32[]{:S(2)}) copy-start(bf16[32,40,384]{2,1,0:T(8,128)(2,1)S(1)} %all-to-all-done.3) | copy-start | bytes 2949124
  212.0 38.4 %all-to-all-start.2 = ((bf16[32,40,512]{2,1,0:T(8,128)(2,1)}), bf16[32,40,512]{2,1,0:T(8,128)(2,1)}, u32[]{:S(2)}, u32[]{:S(2)}) async-start(bf16[32,40,512]{2,1,0:T(8,128)(2,1)} %bitcast.13), calls=%async_computation.2 | async-start | bytes 2621440 | tf_op jit(solution)/shard_map/all_to_all | solution.py:475
  (2 other events, 1.6 us)
